TPU v7x, 256 devices: a whole 4x4x8 slice. The times are simulated.
256 devices in a mesh: depth: 64 (over x_lo, z, y), lat: 4 (over x_hi, core).
Axes of the slice: x: 4 (x_hi: 2, x_lo: 2; x = x_hi * 2 + x_lo), y: 4, z: 8, core: 2. Of those that a mesh axis runs over, the one named last changes fastest.
Arguments:
- incident: float32 [64, 2, 2, 128, 128], P('depth', None, None, 'lat'), may hold values from -6 to 6
- contrast: float32 [64, 128, 128], P('depth', 'lat'), may hold values from -0.8 to 0.8
- kernel: bfloat16 [64, 64, 2, 256, 256], P('depth', None, None, 'lat'), may hold values from -6 to 6
Outputs:
- total_field: float32 [64, 2, 2, 128, 128], P('depth', None, None, 'lat')
All inputs are finite; a program needn't handle non-finite values.
Results may differ from a plain program's by a relative error of at most 0.017.
Values may be sent and summed in bfloat16 or wider, within the bound.
No kernel may reach another device: no remote copies, remote signals or barrier semaphores. Data moves between devices by JAX's collectives and lax.ppermute only.
A program may use at most 64 MiB of HBM per device.

v0:
```python
import math

import jax
import jax.numpy as jnp
from jax import lax
from jax.sharding import PartitionSpec as P

L = 128
ITERS = 3


def wave_tables(count_in, count_out, period):
    indices = (
        jnp.arange(count_in, dtype=jnp.int32)[:, None]
        * jnp.arange(count_out, dtype=jnp.int32)[None, :]
        % period
    )
    angles = indices.astype(jnp.float32) * (2.0 * math.pi / period)
    return (jnp.cos(angles).astype(jnp.bfloat16), jnp.sin(angles).astype(jnp.bfloat16))


def last_dot(left, right):
    return jnp.einsum("...a,ab->...b", left, right, preferred_element_type=jnp.float32)


def middle_dot(left, right):
    return jnp.einsum("...ak,ab->...kb", left, right, preferred_element_type=jnp.float32)


def forward_pass(values, cosine, sine_table, product):
    real_part = values[..., 0, :, :]
    imag_part = values[..., 1, :, :]
    out_real = product(real_part, cosine) + product(imag_part, sine_table)
    out_imag = product(imag_part, cosine) - product(real_part, sine_table)
    return jnp.stack([out_real, out_imag], axis=-3)


def inverse_pass(values, cosine, sine_table, product):
    real_part = values[..., 0, :, :]
    imag_part = values[..., 1, :, :]
    out_real = product(real_part, cosine) - product(imag_part, sine_table)
    out_imag = product(real_part, sine_table) + product(imag_part, cosine)
    return jnp.stack([out_real, out_imag], axis=-3)


def couple_grid(kern_rows, spectra):
    form = "lwkm,wskm->lskm"
    kern_real = kern_rows[:, :, 0]
    kern_imag = kern_rows[:, :, 1]
    spec_real = spectra[:, :, 0]
    spec_imag = spectra[:, :, 1]
    out_real = jnp.einsum(
        form, kern_real, spec_real, preferred_element_type=jnp.float32
    ) - jnp.einsum(form, kern_imag, spec_imag, preferred_element_type=jnp.float32)
    out_imag = jnp.einsum(
        form, kern_real, spec_imag, preferred_element_type=jnp.float32
    ) + jnp.einsum(form, kern_imag, spec_real, preferred_element_type=jnp.float32)
    return jnp.stack([out_real, out_imag], axis=2)


def local(incident, contrast, kernel):
    period = 2 * L
    forward_cos, forward_sin = wave_tables(L, period, period)
    inverse_cos, inverse_sin = wave_tables(period, L, period)
    fields = incident
    for iteration in range(ITERS):
        sources = (contrast[:, None, None] * fields).astype(jnp.bfloat16)
        along_y = forward_pass(sources, forward_cos, forward_sin, last_dot).astype(jnp.bfloat16)
        spectra = forward_pass(
            lax.all_to_all(along_y, "lat", split_axis=4, concat_axis=3, tiled=True),
            forward_cos,
            forward_sin,
            middle_dot,
        ).astype(jnp.bfloat16)
        summed = couple_grid(kernel, lax.all_gather(spectra, "depth", axis=0, tiled=True))
        scattered = summed.astype(jnp.bfloat16)
        along_x = inverse_pass(scattered, inverse_cos, inverse_sin, last_dot).astype(jnp.bfloat16)
        returned = inverse_pass(
            lax.all_to_all(along_x, "lat", split_axis=4, concat_axis=3, tiled=True),
            inverse_cos,
            inverse_sin,
            middle_dot,
        )
        fields = incident + returned / float(period * period)
    return fields


def solution(mesh):
    in_specs = (
        P("depth", None, None, "lat", None),
        P("depth", "lat", None),
        P("depth", None, None, "lat", None),
    )
    out_specs = P("depth", None, None, "lat", None)
    return jax.shard_map(local, mesh=mesh, in_specs=in_specs, out_specs=out_specs, check_vma=False)
```

profile of v0, /device:TPU:1, one launch (start us, length us, event | category | flops | bytes accessed | tf_op | source)
XLA Modules:
  0.0 1056.8 jit_solution(12205641947901959404)
XLA Ops:
  6.5 0.8 multiply_convert_fusion
  10.4 10.4 all_to_all.108
  21.7 0.6 fusion.149
  22.4 0.6 fusion.22
  23.0 0.6 fusion.23
  23.7 0.6 copy.40
  24.4 6.6 bitcast_convert_fusion.1
  30.9 266.8 %all-gather.4.cloned.1.call-done = bf16[64,2,2,64,256]{4,3,2,1,0:T(8,128)(2,1)} async-done(((bf16[1,2,2,64,256]{4,3,2,1,0:T(8,128)(2,1)}), bf16[64,2,2,64,256]{4,3,2,1,0:T(8,128)(2,1)}) %all-gather.4.cloned.1.call-update) | async-done | bytes 8388624 | tf_op jit(solution)/shard_map/all_gather | solution.py:75
  297.8 7.5 fusion.1
  305.4 0.6 fusion.98
  307.3 0.6 fusion.45
  308.2 48.5 %all_to_all.109 = bf16[4,2,4096]{2,1,0:T(2,128)(2,1)S(1)} all-to-all(bf16[4,2,4096]{2,1,0:T(2,128)(2,1)S(1)} %reshape.921), channel_id=1, replica_groups=mesh['depth'=64,'lat'=4] {'lat'}, dimensions={0} | all-to-all | bytes 131072 | tf_op jit(solution)/shard_map/all_to_all | solution.py:79
  362.6 8.0 all_to_all.110
  371.6 0.6 fusion.141
  372.2 0.6 fusion.20
  372.9 0.6 fusion.21
  373.5 0.6 copy.49
  374.3 268.3 %all-gather.6.cloned.1.call-done = bf16[64,2,2,64,256]{4,3,2,1,0:T(8,128)(2,1)} async-done(((bf16[1,2,2,64,256]{4,3,2,1,0:T(8,128)(2,1)}), bf16[64,2,2,64,256]{4,3,2,1,0:T(8,128)(2,1)}) %all-gather.6.cloned.1.call-update) | async-done | bytes 8388624 | tf_op jit(solution)/shard_map/all_gather | solution.py:75
  642.5 7.5 fusion.5
  650.1 0.6 fusion.92
  652.0 0.6 fusion.41
  653.0 48.5 %all_to_all.111 = bf16[4,2,4096]{2,1,0:T(2,128)(2,1)S(1)} all-to-all(bf16[4,2,4096]{2,1,0:T(2,128)(2,1)S(1)} %reshape.925), channel_id=1, replica_groups=mesh['depth'=64,'lat'=4] {'lat'}, dimensions={0} | all-to-all | bytes 131072 | tf_op jit(solution)/shard_map/all_to_all | solution.py:79
  707.4 8.0 all_to_all.112
  717.0 0.6 fusion.18
  717.6 0.6 fusion.19
  718.3 0.6 copy.58
  719.0 268.3 %all-gather.8.cloned.1.call-done = bf16[64,2,2,64,256]{4,3,2,1,0:T(8,128)(2,1)} async-done(((bf16[1,2,2,64,256]{4,3,2,1,0:T(8,128)(2,1)}), bf16[64,2,2,64,256]{4,3,2,1,0:T(8,128)(2,1)}) %all-gather.8.cloned.1.call-update) | async-done | bytes 8388624 | tf_op jit(solution)/shard_map/all_gather | solution.py:75
  987.3 7.5 fusion.9
  994.8 0.6 fusion.86
  996.8 0.6 fusion.37
  997.7 48.6 %all_to_all.113 = bf16[4,2,4096]{2,1,0:T(2,128)(2,1)S(1)} all-to-all(bf16[4,2,4096]{2,1,0:T(2,128)(2,1)S(1)} %reshape.929), channel_id=1, replica_groups=mesh['depth'=64,'lat'=4] {'lat'}, dimensions={0} | all-to-all | bytes 131072 | tf_op jit(solution)/shard_map/all_to_all | solution.py:79
  1049.2 0.6 copy.63
  (91 shorter events, 26.0 us)
Async XLA Ops:
  6.5 291.2 %all-gather.4.cloned.1.call-start = ((), (), s32[]{:S(2)}) async-start(), calls=%async_computation.6 | async-start | bytes 8519680 | tf_op jit(solution)/shard_map/all_gather | solution.py:75
  24.3 618.2 %all-gather.6.cloned.1.call-start = ((), (), s32[]{:S(2)}) async-start(), calls=%async_computation.7 | async-start | bytes 8519680 | tf_op jit(solution)/shard_map/all_gather | solution.py:75
  297.8 61.8 %copy-start = (f32[1,2,2,32,128]{4,3,2,1,0:T(8,128)S(1)}, f32[1,2,2,32,128]{4,3,2,1,0:T(8,128)}, u32[]{:S(2)}) copy-start(f32[1,2,2,32,128]{4,3,2,1,0:T(8,128)} %param.3) | copy-start | bytes 196612
  297.8 61.8 %copy-start.1 = (f32[1,32,128]{2,1,0:T(8,128)S(1)}, f32[1,32,128]{2,1,0:T(8,128)}, u32[]{:S(2)}) copy-start(f32[1,32,128]{2,1,0:T(8,128)} %param.4) | copy-start | bytes 49156
  374.2 613.1 %all-gather.8.cloned.1.call-start = ((), (), s32[]{:S(2)}) async-start(), calls=%async_computation.8 | async-start | bytes 8519680 | tf_op jit(solution)/shard_map/all_gather | solution.py:75
Sparse Core Ops, SparseCore 0:
  24.5 273.2 all-gather.3
  374.3 268.1 all-gather.5
  719.1 268.1 all-gather.7
where the time goes:
time: 1060 us
  waiting for transfers between devices  803 us (76%)
  blocking collectives  172 us (16%)
  other arithmetic  30.3 us (3%)
  matrix products  30 us (3%)
  between operations  14 us (1%)
    all_gather x3, waiting for transfers between devices, local(): lax.all_gather(spectra, 'depth', axis=0, tiled=True)  803 us
    all_to_all x3, blocking collectives, local(): lax.all_to_all(along_x, 'lat', split_axis=4, concat_axis=3, tiled=True)  146 us
    all_to_all x3, blocking collectives, local(): lax.all_to_all(along_y, 'lat', split_axis=4, concat_axis=3, tiled=True)  26.3 us
    dot_general x3, other arithmetic, couple_grid(): jnp.einsum(form, kern_imag, spec_real, preferred_element_type=jnp.float32)  22.6 us
  transfers between devices with their start and end apart: 3, of which 3 were waited for; matrix products, arithmetic and copies ran while one was open for 1% of the time, Pallas kernels for 0%

commit v1 on v0

v1 whole, which is shorter than its diff:
```python
import functools
import itertools
import math

import jax
import jax.numpy as jnp
import ml_dtypes
import numpy as np
from jax import lax
from jax.experimental import pallas as pl
from jax.experimental.pallas import tpu as pltpu
from jax.sharding import Mesh, PartitionSpec as P

L = 128
P_SIZE = 256
NZ = 64
SRC = 2
ITERS = 3
LATS = 4
SHARES = 8
KYS = P_SIZE // (LATS * SHARES)
XS = L // LATS
LANES = SRC * 2 * XS
SPEC = SRC * 2 * P_SIZE

NAMES = ("xl", "zh", "zl", "yh", "yl", "xh", "c")
SIZES = (2, 4, 2, 2, 2, 2, 2)
DEPTH = ("xl", "zh", "zl", "yh", "yl")
LAT = ("xh", "c")
SHARE = ("xl", "zl", "yl")


def bf16(array):
    return np.asarray(array, np.float32).astype(ml_dtypes.bfloat16)


def wave_tables(count_in, count_out):
    index = np.arange(count_in)[:, None] * np.arange(count_out)[None, :] % P_SIZE
    angles = index * (2.0 * math.pi / P_SIZE)
    return np.cos(angles), np.sin(angles)


def tables():
    cosine, sine = wave_tables(L, P_SIZE)
    fwd_y = np.concatenate([cosine.T, sine.T], axis=1)
    fwd_x = np.zeros((LATS, SRC, 2, XS, SRC, 2, P_SIZE))
    cos_x = cosine.reshape(LATS, XS, P_SIZE)
    sin_x = sine.reshape(LATS, XS, P_SIZE)
    for s in range(SRC):
        fwd_x[:, s, 0, :, s, 0] = cos_x
        fwd_x[:, s, 1, :, s, 0] = sin_x
        fwd_x[:, s, 0, :, s, 1] = -sin_x
        fwd_x[:, s, 1, :, s, 1] = cos_x
    inv_cos, inv_sin = wave_tables(P_SIZE, L)
    inv_x = np.zeros((SRC, 2, P_SIZE, LATS, SRC, 2, XS))
    icos_x = inv_cos.reshape(P_SIZE, LATS, XS)
    isin_x = inv_sin.reshape(P_SIZE, LATS, XS)
    for s in range(SRC):
        inv_x[s, 0, :, :, s, 0] = icos_x
        inv_x[s, 1, :, :, s, 0] = -isin_x
        inv_x[s, 0, :, :, s, 1] = isin_x
        inv_x[s, 1, :, :, s, 1] = icos_x
    inv_y = np.concatenate([inv_cos, inv_sin], axis=1)
    return (
        bf16(fwd_y),
        bf16(fwd_x.reshape(LATS * LANES, SPEC)),
        bf16(inv_x.reshape(SPEC, LATS * LANES)),
        bf16(inv_y),
    )


def send_sources(field_parts, contrast_ref, table_ref, out_ref):
    left, right = [], []
    for real_part, imag_part in field_parts:
        real_src = contrast_ref[...] * real_part
        imag_src = contrast_ref[...] * imag_part
        left += [real_src, imag_src]
        right += [imag_src, -real_src]
    both = jnp.concatenate(
        [jnp.concatenate(left, axis=0), jnp.concatenate(right, axis=0)], axis=1
    ).astype(jnp.bfloat16)
    along_y = lax.dot_general(
        table_ref[...], both, (((1,), (1,)), ((), ())), preferred_element_type=jnp.float32
    ).astype(jnp.bfloat16)
    pair = 2 * KYS
    for lat, xl, zh, zl, yh in itertools.product(
        range(LATS), range(2), range(4), range(2), range(2)
    ):
        src = ((lat * 2 + xl) * 2 + zl) * pair
        dst = ((((lat * 2 + xl) * 4 + zh) * 2 + zl) * 2 + yh) * pair
        out_ref[dst : dst + pair, :] = along_y[src : src + pair, :]


def first_body(incident_ref, contrast_ref, table_ref, out_ref):
    parts = [(incident_ref[s, 0], incident_ref[s, 1]) for s in range(SRC)]
    send_sources(parts, contrast_ref, table_ref, out_ref)


def field_of(recv_ref, incident_ref, inv_ref):
    waves = lax.dot_general(
        recv_ref[...], inv_ref[...], (((0,), (0,)), ((), ())),
        preferred_element_type=jnp.float32,
    )
    scale = 1.0 / float(P_SIZE * P_SIZE)
    parts = []
    for s in range(SRC):
        real_rows = waves[2 * s * XS : (2 * s + 1) * XS]
        imag_rows = waves[(2 * s + 1) * XS : (2 * s + 2) * XS]
        parts.append(
            (
                incident_ref[s, 0] + (real_rows[:, :L] - imag_rows[:, L:]) * scale,
                incident_ref[s, 1] + (real_rows[:, L:] + imag_rows[:, :L]) * scale,
            )
        )
    return parts


def next_body(recv_ref, incident_ref, contrast_ref, inv_ref, table_ref, out_ref):
    send_sources(field_of(recv_ref, incident_ref, inv_ref), contrast_ref, table_ref, out_ref)


def last_body(recv_ref, incident_ref, inv_ref, out_ref):
    for s, parts in enumerate(field_of(recv_ref, incident_ref, inv_ref)):
        for part in range(2):
            out_ref[s, part] = parts[part]


BLOCK = 4


def couple_body(me_ref, recv_ref, fwd_ref, inv_ref, *refs):
    kern_refs, out_ref, spec_ref, sum_ref = refs[:SHARES], *refs[SHARES:]
    rows = NZ * KYS
    half = 2 * LANES
    chunk = 128
    for start in range(0, rows, chunk):
        total = None
        for pair in range(LATS // 2):
            left = jnp.concatenate(
                [
                    recv_ref[(2 * pair + i) * rows + start : (2 * pair + i) * rows + start + chunk, :]
                    for i in range(2)
                ],
                axis=1,
            )
            part = jnp.dot(
                left,
                fwd_ref[pair * half : (pair + 1) * half, :],
                preferred_element_type=jnp.float32,
            )
            total = part if total is None else total + part
        spec_ref[start : start + chunk, :] = total.astype(jnp.bfloat16).astype(jnp.float32)

    for first in range(0, SHARES, BLOCK):

        def step(w, sums):
            spec = spec_ref[pl.ds(pl.multiple_of(w * KYS, KYS), KYS), :]
            out = []
            for j in range(BLOCK):
                kern = kern_refs[first + j][w].astype(jnp.float32)
                kern_real, kern_imag = kern[:KYS], kern[KYS:]
                for s in range(SRC):
                    at = 2 * s * P_SIZE
                    spec_real = spec[:, at : at + P_SIZE]
                    spec_imag = spec[:, at + P_SIZE : at + 2 * P_SIZE]
                    real_sum, imag_sum = sums[2 * (j * SRC + s)], sums[2 * (j * SRC + s) + 1]
                    out.append(real_sum + kern_real * spec_real - kern_imag * spec_imag)
                    out.append(imag_sum + kern_real * spec_imag + kern_imag * spec_real)
            return tuple(out)

        zero = jnp.zeros((KYS, P_SIZE), jnp.float32)
        sums = lax.fori_loop(0, NZ, step, (zero,) * (BLOCK * SRC * 2), unroll=2)
        for j in range(BLOCK):
            row = pl.multiple_of((me_ref[0] ^ (first + j)) * KYS, KYS)
            for n in range(2 * SRC):
                sum_ref[pl.ds(row, KYS), n * P_SIZE : (n + 1) * P_SIZE] = sums[
                    j * 2 * SRC + n
                ]

    along_x = jnp.dot(
        sum_ref[...].astype(jnp.bfloat16), inv_ref[...], preferred_element_type=jnp.float32
    ).astype(jnp.bfloat16)
    held = SHARES * KYS
    for lat in range(LATS):
        out_ref[lat * held : (lat + 1) * held, :] = along_x[:, lat * LANES : (lat + 1) * LANES]


VMEM = pl.BlockSpec(memory_space=pltpu.VMEM)
SMEM = pl.BlockSpec(memory_space=pltpu.SMEM)
ALL_ROWS = LATS * NZ * KYS


def call(body, out, args, specs=None, scratch=(), flops=0):
    size = sum(math.prod(a.shape) * a.dtype.itemsize for a in args)
    return pl.pallas_call(
        body,
        out_shape=out,
        in_specs=specs or [VMEM] * len(args),
        out_specs=VMEM,
        scratch_shapes=list(scratch),
        compiler_params=pltpu.CompilerParams(vmem_limit_bytes=24 * 1024 * 1024),
        cost_estimate=pl.CostEstimate(flops=flops, bytes_accessed=size, transcendentals=0),
    )(*args)


def swap_perm(offset):
    pairs = []
    for place in range(SHARES):
        pairs.append((place, place ^ offset))
    return pairs


def local(incident, contrast, kernel):
    fwd_y, fwd_x, inv_x, inv_y = (jnp.asarray(t) for t in tables())
    incident = incident[0]
    contrast = contrast[0]
    me = lax.axis_index(SHARE).astype(jnp.int32)
    kern = kernel[0].reshape(NZ, 2, SHARES, KYS, P_SIZE)

    with jax.named_scope("kernel_exchange"):
        slabs = []
        for offset in range(SHARES):
            piece = lax.dynamic_index_in_dim(kern, me ^ offset, axis=2, keepdims=False)
            piece = piece.reshape(NZ, 2 * KYS, P_SIZE)
            if offset:
                piece = lax.ppermute(piece, SHARE, swap_perm(offset))
            slabs.append(piece)

    send_shape = jax.ShapeDtypeStruct((ALL_ROWS, LANES), jnp.bfloat16)
    back_shape = jax.ShapeDtypeStruct((LATS * SHARES * KYS, LANES), jnp.bfloat16)
    field_shape = jax.ShapeDtypeStruct((SRC, 2, XS, L), jnp.float32)
    sent = call(first_body, send_shape, (incident, contrast, fwd_y), flops=10**7)
    for iteration in range(ITERS):
        with jax.named_scope("to_wavenumbers"):
            got = lax.all_to_all(sent, LAT + DEPTH, 0, 0, tiled=True)
        back = call(
            couple_body,
            back_shape,
            (me.reshape(1), got, fwd_x, inv_x, *slabs),
            specs=[SMEM] + [VMEM] * (3 + SHARES),
            scratch=[
                pltpu.VMEM((NZ * KYS, SPEC), jnp.float32),
                pltpu.VMEM((SHARES * KYS, SPEC), jnp.float32),
            ],
            flops=10**9,
        )
        with jax.named_scope("to_rows"):
            rows = lax.all_to_all(back, LAT + SHARE, 0, 0, tiled=True)
        if iteration < ITERS - 1:
            sent = call(
                next_body, send_shape, (rows, incident, contrast, inv_y, fwd_y), flops=10**7
            )
    fields = call(last_body, field_shape, (rows, incident, inv_y), flops=10**7)
    return fields[None]


def solution(mesh):
    fine = Mesh(mesh.devices.reshape(SIZES), NAMES)
    in_specs = (
        P(DEPTH, None, None, LAT, None),
        P(DEPTH, LAT, None),
        P(DEPTH, None, None, LAT, None),
    )
    out_specs = P(DEPTH, None, None, LAT, None)
    return jax.shard_map(local, mesh=fine, in_specs=in_specs, out_specs=out_specs, check_vma=False)
```

time: 1060 us -> 189 us (0.18)
  waiting for transfers between devices: 803 us -> 39 us
  blocking collectives: 172 us -> 93.7 us
  other arithmetic: 30.3 us -> 0 us
  matrix products: 30 us -> 0 us
  starting transfers between devices: 0.09 us -> 24.3 us
  Pallas kernels: 0 us -> 17.3 us
  between operations: 14 us -> 0.13 us
    all_gather x3 -> x0, waiting for transfers between devices: 803 us -> none  [local(): lax.all_gather(spectra, 'depth', axis=0, tiled=True)]
    all_to_all x6 -> x5, blocking collectives: 172 us -> 93.7 us  [the longest x2 58.8 us: local(): got = lax.all_to_all(sent, LAT + DEPTH, 0, 0, tiled=True)]
    ppermute x0 -> x7, waiting for transfers between devices: none -> 39 us  [local(): piece = lax.ppermute(piece, SHARE, swap_perm(offset))]
    dot_general x48 -> x0, matrix products: 30 us -> none  [the longest x24 15 us: middle_dot(): jnp.einsum('...ak,ab->...kb', left, right, preferred_element_type=jnp.flo...]
    dot_general x3 -> x0, other arithmetic: 22.6 us -> none  [couple_grid(): jnp.einsum(form, kern_imag, spec_real, preferred_element_type=jnp.float32)]
    pallas_call x0 -> x7, Pallas kernels: none -> 17.3 us  [call(): pl.pallas_call(body, out_shape=out, in_specs=specs or [VMEM] * len(args),...]
    all_to_all x0 -> x1, starting transfers between devices: none -> 15.9 us  [local(): got = lax.all_to_all(sent, LAT + DEPTH, 0, 0, tiled=True)]
  transfers between devices with their start and end apart: 3 -> 8, of which waited for: 3 -> 4; matrix products, arithmetic and copies ran while one was open for 1% -> 0% of each run, Pallas kernels for 0% -> 0%
where the time goes in v1:
time: 189 us
  blocking collectives  93.7 us (50%)
  waiting for transfers between devices  39 us (21%)
  starting transfers between devices  24.3 us (13%)
  Pallas kernels  17.3 us (9%)
  local copies, waits for them, and re-layouts  14.2 us (8%)
    all_to_all x2, blocking collectives, local(): got = lax.all_to_all(sent, LAT + DEPTH, 0, 0, tiled=True)  58.8 us
    ppermute x7, waiting for transfers between devices, local(): piece = lax.ppermute(piece, SHARE, swap_perm(offset))  39 us
    all_to_all x3, blocking collectives, local(): rows = lax.all_to_all(back, LAT + SHARE, 0, 0, tiled=True)  34.9 us
    pallas_call x7, Pallas kernels, call(): pl.pallas_call(body, out_shape=out, in_specs=specs or [VMEM] * len(args),...  17.3 us
    all_to_all x1, starting transfers between devices, local(): got = lax.all_to_all(sent, LAT + DEPTH, 0, 0, tiled=True)  15.9 us
    unnamed x36, local copies, waits for them, and re-layouts  9.99 us
    ppermute x7, starting transfers between devices, local(): piece = lax.ppermute(piece, SHARE, swap_perm(offset))  8.44 us
    reshape x1, local copies, waits for them, and re-layouts, local(): piece = piece.reshape(NZ, 2 * KYS, P_SIZE)  4.24 us
  transfers between devices with their start and end apart: 8, of which 4 were waited for; matrix products, arithmetic and copies ran while one was open for 0% of the time, Pallas kernels for 0%

profile of v1, /device:TPU:1, one launch (start us, length us, event | category | flops | bytes accessed | tf_op | source)
XLA Modules:
  0.0 188.7 jit_solution(5455419503933322110)
XLA Ops:
  0.0 4.2 %dynamic-slice_bitcast_fusion = (bf16[64,16,256]{2,1,0:T(8,128)(2,1)}, bf16[64,16,256]{2,1,0:T(8,128)(2,1)}, bf16[64,16,256]{2,1,0:T(8,128)(2,1)}, bf16[64,16,25...) fusion(bf16[64,2,8,8,256]{4,3,2,1,0:T(8,128)(2,1)} %bitcast.67,, ...), kind=kLoop, calls=%fused_computation | loop fusion | bytes 8388640 | tf_op jit(solution)/shard_map/kernel_exchange/reshape | solution.py:224
  4.3 4.4 %collective-permute-start.6 = (bf16[64,16,256]{2,1,0:T(8,128)(2,1)}, bf16[64,16,256]{2,1,0:T(8,128)(2,1)S(1)}, u32[]{:S(2)}, u32[]{:S(2)}) collective-permute-start(bf16[64,16,256]{2,1,0:T(8,128)(2,1)} %get-tuple-element.5), channel_id=1, source_target_pairs={{0,148},{4,144},{16,132},{20,128},{128,20},{132,16},{144,4},{148,0... | collective-permute-start | bytes 1572872 | tf_op jit(solution)/shard_map/kernel_exchange/ppermute | solution.py:226
  8.9 0.8 copy-done.15
  9.7 15.9 %all-to-all-start = ((bf16[256,8,128]{2,1,0:T(8,128)(2,1)}), bf16[256,8,128]{2,1,0:T(8,128)(2,1)}, u32[]{:S(2)}, u32[]{:S(2)}) async-start(bf16[256,8,128]{2,1,0:T(8,128)(2,1)} %bitcast.51), calls=%async_computation | async-start | bytes 1048576 | tf_op jit(solution)/shard_map/to_wavenumbers/all_to_all | solution.py:235
  25.6 2.4 %collective-permute-start.4 = (bf16[64,16,256]{2,1,0:T(8,128)(2,1)}, bf16[64,16,256]{2,1,0:T(8,128)(2,1)S(1)}, u32[]{:S(2)}, u32[]{:S(2)}) collective-permute-start(bf16[64,16,256]{2,1,0:T(8,128)(2,1)} %get-tuple-element.7), channel_id=1, source_target_pairs={{0,132},{4,128},{16,148},{20,144},{128,4},{132,0},{144,20},{148,16... | collective-permute-start | bytes 1572872 | tf_op jit(solution)/shard_map/kernel_exchange/ppermute | solution.py:226
  28.0 0.3 collective-permute-start.3
  28.3 1.3 collective-permute-start.2
  29.6 4.9 %collective-permute-done.5.refs_6_ = bf16[64,16,256]{2,1,0:T(8,128)(2,1)} collective-permute-done((bf16[64,16,256]{2,1,0:T(8,128)(2,1)}, bf16[64,16,256]{2,1,0:T(8,128)(2,1)}, u32[]{:S(2)}, u32[]{:S(2)}) %collective-permute-start.5) | collective-permute-done | bytes 524320 | tf_op jit(solution)/shard_map/kernel_exchange/ppermute | solution.py:226
  34.5 19.7 %collective-permute-done.4.refs_5_ = bf16[64,16,256]{2,1,0:T(8,128)(2,1)S(1)} collective-permute-done((bf16[64,16,256]{2,1,0:T(8,128)(2,1)}, bf16[64,16,256]{2,1,0:T(8,128)(2,1)S(1)}, u32[]{:S(2)}, u32[]{:S(2)}) %collective-permute-start.4) | collective-permute-done | bytes 524320 | tf_op jit(solution)/shard_map/kernel_exchange/ppermute | solution.py:226
  54.2 0.8 copy-done.3
  55.0 10.5 %collective-permute-done.3.refs_4_ = bf16[64,16,256]{2,1,0:T(8,128)(2,1)S(1)} collective-permute-done((bf16[64,16,256]{2,1,0:T(8,128)(2,1)}, bf16[64,16,256]{2,1,0:T(8,128)(2,1)S(1)}, u32[]{:S(2)}, u32[]{:S(2)}) %collective-permute-start.3) | collective-permute-done | bytes 524320 | tf_op jit(solution)/shard_map/kernel_exchange/ppermute | solution.py:226
  65.5 0.8 copy-done.6
  66.3 0.8 copy-done.8
  67.1 4.0 %collective-permute-done.1.refs_2_ = bf16[64,16,256]{2,1,0:T(8,128)(2,1)S(1)} collective-permute-done((bf16[64,16,256]{2,1,0:T(8,128)(2,1)}, bf16[64,16,256]{2,1,0:T(8,128)(2,1)S(1)}, u32[]{:S(2)}, u32[]{:S(2)}) %collective-permute-start.1) | collective-permute-done | bytes 524320 | tf_op jit(solution)/shard_map/kernel_exchange/ppermute | solution.py:226
  71.1 0.8 copy-done.10
  71.9 0.8 copy-done.12
  72.7 1.0 copy-done.4
  73.7 1.0 copy-done.7
  74.7 1.0 copy-done.9
  75.8 1.0 copy-done.11
  76.8 1.0 copy-done.13
  77.9 5.3 %shard_map.74 = bf16[256,128]{1,0:T(8,128)(2,1)S(1)} custom-call(s32[1]{0:T(128)} %bitcast.me_ref, bf16[2048,128]{1,0:T(8,128)(2,1)} %bitcast.4.recv_ref, bf16[512,1024]{1,0:T(8,128)(2,1)S(1)} %copy-done.1, bf16[1024,512]{1,0:T(8,128)(2,1)S(1)} %copy-done, bf16[64,16,256]{2,1,0:T(8,128)(2,1)S(1)} %get-tuple-element.12.refs_0_, ...), custom_call_target="tpu_custom_call" | custom-call | flops 1000000000 | bytes 6815748 | tf_op jit(solution)/shard_map/pallas_call | solution.py:195
  83.2 13.6 %all_to_all.66 = bf16[32,8,128]{2,1,0:T(8,128)(2,1)S(1)} all-to-all(bf16[32,8,128]{2,1,0:T(8,128)(2,1)S(1)} %bitcast.59), channel_id=1, replica_groups=mesh['xl'=2,'zh'=4,'zl'=2,'yh'=2,'yl'=2,'xh'=2,'c'=2] {'xh','c','xl','zl..., dimensions={0} | all-to-all | bytes 131072 | tf_op jit(solution)/shard_map/to_rows/all_to_all | solution.py:248
  96.8 0.4 shard_map.75
  97.2 32.6 %all_to_all.67 = bf16[256,8,128]{2,1,0:T(8,128)(2,1)S(1)} all-to-all(bf16[256,8,128]{2,1,0:T(8,128)(2,1)S(1)} %bitcast.49), channel_id=1, replica_groups=mesh['xl'=2,'zh'=4,'zl'=2,'yh'=2,'yl'=2,'xh'=2,'c'=2] {'xh','c','xl','zh..., dimensions={0} | all-to-all | bytes 1048576 | tf_op jit(solution)/shard_map/to_wavenumbers/all_to_all | solution.py:235
  129.7 5.1 %shard_map.76 = bf16[256,128]{1,0:T(8,128)(2,1)S(1)} custom-call(s32[1]{0:T(128)} %bitcast.me_ref, bf16[2048,128]{1,0:T(8,128)(2,1)S(1)} %bitcast.53, bf16[512,1024]{1,0:T(8,128)(2,1)S(1)} %copy-done.1, bf16[1024,512]{1,0:T(8,128)(2,1)S(1)} %copy-done, bf16[64,16,256]{2,1,0:T(8,128)(2,1)S(1)} %get-tuple-element.12.refs_0_, ...), custom_call_target="tpu_custom_call" | custom-call | flops 1000000000 | bytes 6815748 | tf_op jit(solution)/shard_map/pallas_call | solution.py:195
  134.8 10.6 %all_to_all.68 = bf16[32,8,128]{2,1,0:T(8,128)(2,1)S(1)} all-to-all(bf16[32,8,128]{2,1,0:T(8,128)(2,1)S(1)} %bitcast.60), channel_id=1, replica_groups=mesh['xl'=2,'zh'=4,'zl'=2,'yh'=2,'yl'=2,'xh'=2,'c'=2] {'xh','c','xl','zl..., dimensions={0} | all-to-all | bytes 131072 | tf_op jit(solution)/shard_map/to_rows/all_to_all | solution.py:248
  145.5 0.4 shard_map.77
  145.9 26.2 %all_to_all.69 = bf16[256,8,128]{2,1,0:T(8,128)(2,1)S(1)} all-to-all(bf16[256,8,128]{2,1,0:T(8,128)(2,1)S(1)} %bitcast.50), channel_id=1, replica_groups=mesh['xl'=2,'zh'=4,'zl'=2,'yh'=2,'yl'=2,'xh'=2,'c'=2] {'xh','c','xl','zh..., dimensions={0} | all-to-all | bytes 1048576 | tf_op jit(solution)/shard_map/to_wavenumbers/all_to_all | solution.py:235
  172.1 5.1 %shard_map.78 = bf16[256,128]{1,0:T(8,128)(2,1)S(1)} custom-call(s32[1]{0:T(128)} %bitcast.me_ref, bf16[2048,128]{1,0:T(8,128)(2,1)S(1)} %bitcast.52, bf16[512,1024]{1,0:T(8,128)(2,1)S(1)} %copy-done.1, bf16[1024,512]{1,0:T(8,128)(2,1)S(1)} %copy-done, bf16[64,16,256]{2,1,0:T(8,128)(2,1)S(1)} %get-tuple-element.12.refs_0_, ...), custom_call_target="tpu_custom_call" | custom-call | flops 1000000000 | bytes 6815748 | tf_op jit(solution)/shard_map/pallas_call | solution.py:195
  177.2 10.6 %all_to_all.70 = bf16[32,8,128]{2,1,0:T(8,128)(2,1)S(1)} all-to-all(bf16[32,8,128]{2,1,0:T(8,128)(2,1)S(1)} %bitcast.58), channel_id=1, replica_groups=mesh['xl'=2,'zh'=4,'zl'=2,'yh'=2,'yl'=2,'xh'=2,'c'=2] {'xh','c','xl','zl..., dimensions={0} | all-to-all | bytes 131072 | tf_op jit(solution)/shard_map/to_rows/all_to_all | solution.py:248
  187.8 0.8 shard_map.79
  (33 shorter events, 0.3 us)
Async XLA Ops:
  0.0 8.7 %copy-start.2 = (bf16[256,256]{1,0:T(8,128)(2,1)S(1)}, bf16[256,256]{1,0:T(8,128)(2,1)}, u32[]{:S(2)}) copy-start(bf16[256,256]{1,0:T(8,128)(2,1)} %constant.54.clone.table_ref.inv_ref) | copy-start | bytes 393220
  0.0 8.7 %copy-start.16 = (f32[1,2,2,32,128]{4,3,2,1,0:T(8,128)S(1)}, f32[1,2,2,32,128]{4,3,2,1,0:T(8,128)}, u32[]{:S(2)}) copy-start(f32[1,2,2,32,128]{4,3,2,1,0:T(8,128)} %param.7) | copy-start | bytes 196612
  0.0 8.7 %copy-start.17 = (f32[1,32,128]{2,1,0:T(8,128)S(1)}, f32[1,32,128]{2,1,0:T(8,128)}, u32[]{:S(2)}) copy-start(f32[1,32,128]{2,1,0:T(8,128)} %param.8) | copy-start | bytes 49156
  0.0 72.6 %copy-start = (bf16[1024,512]{1,0:T(8,128)(2,1)S(1)}, bf16[1024,512]{1,0:T(8,128)(2,1)}, u32[]{:S(2)}) copy-start(bf16[1024,512]{1,0:T(8,128)(2,1)} %constant.56.clone.inv_ref) | copy-start | bytes 3145732
  0.0 72.6 %copy-start.1 = (bf16[512,1024]{1,0:T(8,128)(2,1)S(1)}, bf16[512,1024]{1,0:T(8,128)(2,1)}, u32[]{:S(2)}) copy-start(bf16[512,1024]{1,0:T(8,128)(2,1)} %constant.55.clone.fwd_ref) | copy-start | bytes 3145732
  4.3 25.3 %collective-permute-start.6 = (bf16[64,16,256]{2,1,0:T(8,128)(2,1)}, bf16[64,16,256]{2,1,0:T(8,128)(2,1)S(1)}, u32[]{:S(2)}, u32[]{:S(2)}) collective-permute-start(bf16[64,16,256]{2,1,0:T(8,128)(2,1)} %get-tuple-element.5), channel_id=1, source_target_pairs={{0,148},{4,144},{16,132},{20,128},{128,20},{132,16},{144,4},{148,0... | collective-permute-start | bytes 1572872 | tf_op jit(solution)/shard_map/kernel_exchange/ppermute | solution.py:226
  8.7 25.8 %collective-permute-start.5 = (bf16[64,16,256]{2,1,0:T(8,128)(2,1)}, bf16[64,16,256]{2,1,0:T(8,128)(2,1)}, u32[]{:S(2)}, u32[]{:S(2)}) collective-permute-start(bf16[64,16,256]{2,1,0:T(8,128)(2,1)} %get-tuple-element.6), channel_id=1, source_target_pairs={{0,144},{4,148},{16,128},{20,132},{128,16},{132,20},{144,0},{148,4... | collective-permute-start | bytes 1572872 | tf_op jit(solution)/shard_map/kernel_exchange/ppermute | solution.py:226
  8.9 0.8 copy-start.15
  9.7 62.9 %all-to-all-start = ((bf16[256,8,128]{2,1,0:T(8,128)(2,1)}), bf16[256,8,128]{2,1,0:T(8,128)(2,1)}, u32[]{:S(2)}, u32[]{:S(2)}) async-start(bf16[256,8,128]{2,1,0:T(8,128)(2,1)} %bitcast.51), calls=%async_computation | async-start | bytes 1048576 | tf_op jit(solution)/shard_map/to_wavenumbers/all_to_all | solution.py:235
  25.6 28.6 %collective-permute-start.4 = (bf16[64,16,256]{2,1,0:T(8,128)(2,1)}, bf16[64,16,256]{2,1,0:T(8,128)(2,1)S(1)}, u32[]{:S(2)}, u32[]{:S(2)}) collective-permute-start(bf16[64,16,256]{2,1,0:T(8,128)(2,1)} %get-tuple-element.7), channel_id=1, source_target_pairs={{0,132},{4,128},{16,148},{20,144},{128,4},{132,0},{144,20},{148,16... | collective-permute-start | bytes 1572872 | tf_op jit(solution)/shard_map/kernel_exchange/ppermute | solution.py:226
  28.0 37.5 %collective-permute-start.3 = (bf16[64,16,256]{2,1,0:T(8,128)(2,1)}, bf16[64,16,256]{2,1,0:T(8,128)(2,1)S(1)}, u32[]{:S(2)}, u32[]{:S(2)}) collective-permute-start(bf16[64,16,256]{2,1,0:T(8,128)(2,1)} %get-tuple-element.8), channel_id=1, source_target_pairs={{0,128},{4,132},{16,144},{20,148},{128,0},{132,4},{144,16},{148,20... | collective-permute-start | bytes 1572872 | tf_op jit(solution)/shard_map/kernel_exchange/ppermute | solution.py:226
  28.3 38.0 %collective-permute-start.2 = (bf16[64,16,256]{2,1,0:T(8,128)(2,1)}, bf16[64,16,256]{2,1,0:T(8,128)(2,1)S(1)}, u32[]{:S(2)}, u32[]{:S(2)}) collective-permute-start(bf16[64,16,256]{2,1,0:T(8,128)(2,1)} %get-tuple-element.9), channel_id=1, source_target_pairs={{0,20},{4,16},{16,4},{20,0},{128,148},{132,144},{144,132},{148,128... | collective-permute-start | bytes 1572872 | tf_op jit(solution)/shard_map/kernel_exchange/ppermute | solution.py:226
  29.6 41.5 %collective-permute-start.1 = (bf16[64,16,256]{2,1,0:T(8,128)(2,1)}, bf16[64,16,256]{2,1,0:T(8,128)(2,1)S(1)}, u32[]{:S(2)}, u32[]{:S(2)}) collective-permute-start(bf16[64,16,256]{2,1,0:T(8,128)(2,1)} %get-tuple-element.10), channel_id=1, source_target_pairs={{0,16},{4,20},{16,0},{20,4},{128,144},{132,148},{144,128},{148,132... | collective-permute-start | bytes 1572872 | tf_op jit(solution)/shard_map/kernel_exchange/ppermute | solution.py:226
  34.5 37.3 %collective-permute-start = (bf16[64,16,256]{2,1,0:T(8,128)(2,1)}, bf16[64,16,256]{2,1,0:T(8,128)(2,1)S(1)}, u32[]{:S(2)}, u32[]{:S(2)}) collective-permute-start(bf16[64,16,256]{2,1,0:T(8,128)(2,1)} %get-tuple-element.11), channel_id=1, source_target_pairs={{0,4},{4,0},{16,20},{20,16},{128,132},{132,128},{144,148},{148,144... | collective-permute-start | bytes 1572872 | tf_op jit(solution)/shard_map/kernel_exchange/ppermute | solution.py:226
  54.2 0.8 copy-start.3
  65.5 0.8 copy-start.6
  66.3 0.8 copy-start.8
  71.1 0.8 copy-start.10
  71.9 0.8 copy-start.12
  72.7 1.0 copy-start.4
  73.7 1.0 copy-start.7
  74.7 1.0 copy-start.9
  75.8 1.0 copy-start.11
  76.8 1.0 copy-start.13
  77.9 51.9 %copy-start.5 = (bf16[64,16,256]{2,1,0:T(8,128)(2,1)S(1)}, bf16[64,16,256]{2,1,0:T(8,128)(2,1)}, u32[]{:S(2)}) copy-start(bf16[64,16,256]{2,1,0:T(8,128)(2,1)} %copy-done.3) | copy-start | bytes 1572868
  77.9 51.9 %copy-start.14 = (bf16[64,16,256]{2,1,0:T(8,128)(2,1)S(1)}, bf16[64,16,256]{2,1,0:T(8,128)(2,1)}, u32[]{:S(2)}) copy-start(bf16[64,16,256]{2,1,0:T(8,128)(2,1)} %copy-done.12) | copy-start | bytes 1572868

commit v2 on v1

--- a/solution.py
+++ b/solution.py
@@ -1,4 +1,3 @@
-import functools
 import itertools
 import math
 
@@ -125,23 +124,31 @@
             out_ref[s, part] = parts[part]
 
 
-BLOCK = 4
-
-
-def couple_body(me_ref, recv_ref, fwd_ref, inv_ref, *refs):
-    kern_refs, out_ref, spec_ref, sum_ref = refs[:SHARES], *refs[SHARES:]
+SENT = (1, 2, 3, 4, 5, 6, 7)
+COUPLE_MIB = 52
+BLOCK = 2
+
+
+def load_slabs(slab_refs, kern_ref, arrived):
+    copies = [
+        pltpu.make_async_copy(slab, kern_ref.at[n], arrived.at[n])
+        for n, slab in enumerate(slab_refs)
+    ]
+    for copy in copies:
+        copy.start()
+    return copies
+
+
+def transform_x(recv_ref, fwd_ref, spec_ref):
     rows = NZ * KYS
     half = 2 * LANES
     chunk = 128
     for start in range(0, rows, chunk):
         total = None
         for pair in range(LATS // 2):
+            at = 2 * pair * rows + start
             left = jnp.concatenate(
-                [
-                    recv_ref[(2 * pair + i) * rows + start : (2 * pair + i) * rows + start + chunk, :]
-                    for i in range(2)
-                ],
-                axis=1,
+                [recv_ref[at : at + chunk, :], recv_ref[at + rows : at + rows + chunk, :]], axis=1
             )
             part = jnp.dot(
                 left,
@@ -151,13 +158,19 @@
             total = part if total is None else total + part
         spec_ref[start : start + chunk, :] = total.astype(jnp.bfloat16).astype(jnp.float32)
 
-    for first in range(0, SHARES, BLOCK):
-
-        def step(w, sums):
+
+def couple(spec_ref, kern_ref, copies, put):
+    count = len(copies)
+    for first in range(0, count, BLOCK):
+        block = range(first, min(first + BLOCK, count))
+        for n in block:
+            copies[n].wait()
+
+        def step(w, sums, block=block):
             spec = spec_ref[pl.ds(pl.multiple_of(w * KYS, KYS), KYS), :]
             out = []
-            for j in range(BLOCK):
-                kern = kern_refs[first + j][w].astype(jnp.float32)
+            for j, n in enumerate(block):
+                kern = kern_ref[n, w].astype(jnp.float32)
                 kern_real, kern_imag = kern[:KYS], kern[KYS:]
                 for s in range(SRC):
                     at = 2 * s * P_SIZE
@@ -169,14 +182,21 @@
             return tuple(out)
 
         zero = jnp.zeros((KYS, P_SIZE), jnp.float32)
-        sums = lax.fori_loop(0, NZ, step, (zero,) * (BLOCK * SRC * 2), unroll=2)
-        for j in range(BLOCK):
-            row = pl.multiple_of((me_ref[0] ^ (first + j)) * KYS, KYS)
-            for n in range(2 * SRC):
-                sum_ref[pl.ds(row, KYS), n * P_SIZE : (n + 1) * P_SIZE] = sums[
-                    j * 2 * SRC + n
-                ]
-
+        sums = lax.fori_loop(0, NZ, step, (zero,) * (len(block) * SRC * 2), unroll=4)
+        for j, n in enumerate(block):
+            for quarter in range(2 * SRC):
+                put(n, quarter, sums[j * 2 * SRC + quarter])
+
+
+def put_by_place(me_ref, offsets, sum_ref):
+    def put(n, quarter, total):
+        row = pl.multiple_of((me_ref[0] ^ offsets[n]) * KYS, KYS)
+        sum_ref[pl.ds(row, KYS), quarter * P_SIZE : (quarter + 1) * P_SIZE] = total
+
+    return put
+
+
+def invert_x(sum_ref, inv_ref, out_ref):
     along_x = jnp.dot(
         sum_ref[...].astype(jnp.bfloat16), inv_ref[...], preferred_element_type=jnp.float32
     ).astype(jnp.bfloat16)
@@ -185,20 +205,33 @@
         out_ref[lat * held : (lat + 1) * held, :] = along_x[:, lat * LANES : (lat + 1) * LANES]
 
 
+def couple_body(me_ref, recv_hbm, fwd_ref, inv_ref, *refs):
+    slab_refs, refs = refs[:SHARES], refs[SHARES:]
+    out_ref, spec_ref, sum_ref, recv_ref, loaded, kern_ref, arrived = refs
+    recv_copy = pltpu.make_async_copy(recv_hbm, recv_ref, loaded)
+    recv_copy.start()
+    slab_copies = load_slabs(slab_refs, kern_ref, arrived)
+    recv_copy.wait()
+    transform_x(recv_ref, fwd_ref, spec_ref)
+    couple(spec_ref, kern_ref, slab_copies, put_by_place(me_ref, range(SHARES), sum_ref))
+    invert_x(sum_ref, inv_ref, out_ref)
+
+
 VMEM = pl.BlockSpec(memory_space=pltpu.VMEM)
 SMEM = pl.BlockSpec(memory_space=pltpu.SMEM)
+HBM = pl.BlockSpec(memory_space=pltpu.HBM)
 ALL_ROWS = LATS * NZ * KYS
 
 
-def call(body, out, args, specs=None, scratch=(), flops=0):
+def call(body, out, args, specs=None, scratch=(), flops=0, mib=24):
     size = sum(math.prod(a.shape) * a.dtype.itemsize for a in args)
     return pl.pallas_call(
         body,
         out_shape=out,
         in_specs=specs or [VMEM] * len(args),
-        out_specs=VMEM,
+        out_specs=jax.tree.map(lambda _: VMEM, out),
         scratch_shapes=list(scratch),
-        compiler_params=pltpu.CompilerParams(vmem_limit_bytes=24 * 1024 * 1024),
+        compiler_params=pltpu.CompilerParams(vmem_limit_bytes=mib * 1024 * 1024),
         cost_estimate=pl.CostEstimate(flops=flops, bytes_accessed=size, transcendentals=0),
     )(*args)
 
@@ -215,16 +248,15 @@
     incident = incident[0]
     contrast = contrast[0]
     me = lax.axis_index(SHARE).astype(jnp.int32)
+    me = me.reshape(1)
     kern = kernel[0].reshape(NZ, 2, SHARES, KYS, P_SIZE)
 
     with jax.named_scope("kernel_exchange"):
-        slabs = []
-        for offset in range(SHARES):
-            piece = lax.dynamic_index_in_dim(kern, me ^ offset, axis=2, keepdims=False)
+        slabs = [None] * SHARES
+        for offset in (0,) + SENT:
+            piece = lax.dynamic_index_in_dim(kern, me[0] ^ offset, axis=2, keepdims=False)
             piece = piece.reshape(NZ, 2 * KYS, P_SIZE)
-            if offset:
-                piece = lax.ppermute(piece, SHARE, swap_perm(offset))
-            slabs.append(piece)
+            slabs[offset] = lax.ppermute(piece, SHARE, swap_perm(offset)) if offset else piece
 
     send_shape = jax.ShapeDtypeStruct((ALL_ROWS, LANES), jnp.bfloat16)
     back_shape = jax.ShapeDtypeStruct((LATS * SHARES * KYS, LANES), jnp.bfloat16)
@@ -236,13 +268,18 @@
         back = call(
             couple_body,
             back_shape,
-            (me.reshape(1), got, fwd_x, inv_x, *slabs),
-            specs=[SMEM] + [VMEM] * (3 + SHARES),
+            (me, got, fwd_x, inv_x, *slabs),
+            specs=[SMEM, HBM, VMEM, VMEM] + [HBM] * SHARES,
             scratch=[
                 pltpu.VMEM((NZ * KYS, SPEC), jnp.float32),
                 pltpu.VMEM((SHARES * KYS, SPEC), jnp.float32),
+                pltpu.VMEM((ALL_ROWS, LANES), jnp.bfloat16),
+                pltpu.SemaphoreType.DMA,
+                pltpu.VMEM((SHARES, NZ, 2 * KYS, P_SIZE), jnp.bfloat16),
+                pltpu.SemaphoreType.DMA((SHARES,)),
             ],
             flops=10**9,
+            mib=COUPLE_MIB,
         )
         with jax.named_scope("to_rows"):
             rows = lax.all_to_all(back, LAT + SHARE, 0, 0, tiled=True)

time: 189 us -> 184 us (0.974)
  local copies, waits for them, and re-layouts: 14.2 us -> 4.9 us
  waiting for transfers between devices: 39 us -> 42.2 us
  Pallas kernels: 17.3 us -> 19.3 us
    unnamed x36 -> x18, local copies, waits for them, and re-layouts: 9.99 us -> 0.85 us
    ppermute x7, waiting for transfers between devices: 39 us -> 42.2 us  [local(): lax.ppermute(piece, SHARE, swap_perm(offset))]
    pallas_call x7, Pallas kernels: 17.3 us -> 19.3 us  [call(): pl.pallas_call(body, out_shape=out, in_specs=specs or [VMEM] * len(args),...]
  transfers between devices with their start and end apart: 8 -> 8, of which waited for: 4 -> 4; matrix products, arithmetic and copies ran while one was open for 0% -> 0% of each run, Pallas kernels for 0% -> 1%
where the time goes in v2:
time: 184 us
  blocking collectives  93.8 us (51%)
  waiting for transfers between devices  42.2 us (23%)
  starting transfers between devices  23.4 us (13%)
  Pallas kernels  19.3 us (10%)
  local copies, waits for them, and re-layouts  4.9 us (3%)
    all_to_all x2, blocking collectives, local(): got = lax.all_to_all(sent, LAT + DEPTH, 0, 0, tiled=True)  58.8 us
    ppermute x7, waiting for transfers between devices, local(): lax.ppermute(piece, SHARE, swap_perm(offset))  42.2 us
    all_to_all x3, blocking collectives, local(): rows = lax.all_to_all(back, LAT + SHARE, 0, 0, tiled=True)  35 us
    pallas_call x7, Pallas kernels, call(): pl.pallas_call(body, out_shape=out, in_specs=specs or [VMEM] * len(args),...  19.3 us
    all_to_all x1, starting transfers between devices, local(): got = lax.all_to_all(sent, LAT + DEPTH, 0, 0, tiled=True)  14.9 us
    ppermute x7, starting transfers between devices, local(): lax.ppermute(piece, SHARE, swap_perm(offset))  8.53 us
    reshape x1, local copies, waits for them, and re-layouts, local(): piece = piece.reshape(NZ, 2 * KYS, P_SIZE)  4.05 us
  transfers between devices with their start and end apart: 8, of which 4 were waited for; matrix products, arithmetic and copies ran while one was open for 0% of the time, Pallas kernels for 1%

profile of v2, /device:TPU:1, one launch (start us, length us, event | category | flops | bytes accessed | tf_op | source)
XLA Modules:
  0.0 183.6 jit_solution(14373208277707595825)
XLA Ops:
  0.0 4.0 %dynamic-slice_bitcast_fusion = (bf16[64,16,256]{2,1,0:T(8,128)(2,1)}, bf16[64,16,256]{2,1,0:T(8,128)(2,1)S(1)}, bf16[64,16,256]{2,1,0:T(8,128)(2,1)}, bf16[64,1...) fusion(bf16[64,2,8,8,256]{4,3,2,1,0:T(8,128)(2,1)} %bitcast.67,, ...), kind=kLoop, calls=%fused_computation | loop fusion | bytes 8388640 | tf_op jit(solution)/shard_map/kernel_exchange/reshape | solution.py:258
  4.1 4.4 %collective-permute-start.6 = (bf16[64,16,256]{2,1,0:T(8,128)(2,1)}, bf16[64,16,256]{2,1,0:T(8,128)(2,1)S(1)}, u32[]{:S(2)}, u32[]{:S(2)}) collective-permute-start(bf16[64,16,256]{2,1,0:T(8,128)(2,1)} %get-tuple-element.5), channel_id=1, source_target_pairs={{0,148},{4,144},{16,132},{20,128},{128,20},{132,16},{144,4},{148,0... | collective-permute-start | bytes 1572872 | tf_op jit(solution)/shard_map/kernel_exchange/ppermute | solution.py:259
  8.5 0.0 collective-permute-start.5
  8.5 0.0 copy-done
  8.5 0.0 copy-done.1
  8.5 1.0 shard_map.73
  9.5 14.9 %all-to-all-start = ((bf16[256,8,128]{2,1,0:T(8,128)(2,1)}), bf16[256,8,128]{2,1,0:T(8,128)(2,1)S(1)}, u32[]{:S(2)}, u32[]{:S(2)}) async-start(bf16[256,8,128]{2,1,0:T(8,128)(2,1)} %bitcast.3), calls=%async_computation | async-start | bytes 1048576 | tf_op jit(solution)/shard_map/to_wavenumbers/all_to_all | solution.py:267
  24.4 2.4 %collective-permute-start.4 = (bf16[64,16,256]{2,1,0:T(8,128)(2,1)}, bf16[64,16,256]{2,1,0:T(8,128)(2,1)S(1)}, u32[]{:S(2)}, u32[]{:S(2)}) collective-permute-start(bf16[64,16,256]{2,1,0:T(8,128)(2,1)} %get-tuple-element.7), channel_id=1, source_target_pairs={{0,132},{4,128},{16,148},{20,144},{128,4},{132,0},{144,20},{148,16... | collective-permute-start | bytes 1572872 | tf_op jit(solution)/shard_map/kernel_exchange/ppermute | solution.py:259
  26.8 0.3 collective-permute-start.3
  27.0 1.3 collective-permute-start.2
  28.3 0.0 collective-permute-done.6.refs_7_
  28.3 0.2 collective-permute-start.1
  28.5 5.7 %collective-permute-done.5.refs_6_ = bf16[64,16,256]{2,1,0:T(8,128)(2,1)S(1)} collective-permute-done((bf16[64,16,256]{2,1,0:T(8,128)(2,1)S(1)}, bf16[64,16,256]{2,1,0:T(8,128)(2,1)S(1)}, u32[]{:S(2)}, u32[]{:S(2)}) %collective-permute-start.5) | collective-permute-done | bytes 524320 | tf_op jit(solution)/shard_map/kernel_exchange/ppermute | solution.py:259
  34.2 0.0 collective-permute-start
  34.2 19.8 %collective-permute-done.4.refs_5_ = bf16[64,16,256]{2,1,0:T(8,128)(2,1)S(1)} collective-permute-done((bf16[64,16,256]{2,1,0:T(8,128)(2,1)}, bf16[64,16,256]{2,1,0:T(8,128)(2,1)S(1)}, u32[]{:S(2)}, u32[]{:S(2)}) %collective-permute-start.4) | collective-permute-done | bytes 524320 | tf_op jit(solution)/shard_map/kernel_exchange/ppermute | solution.py:259
  54.0 10.4 %collective-permute-done.3.refs_4_ = bf16[64,16,256]{2,1,0:T(8,128)(2,1)S(1)} collective-permute-done((bf16[64,16,256]{2,1,0:T(8,128)(2,1)}, bf16[64,16,256]{2,1,0:T(8,128)(2,1)S(1)}, u32[]{:S(2)}, u32[]{:S(2)}) %collective-permute-start.3) | collective-permute-done | bytes 524320 | tf_op jit(solution)/shard_map/kernel_exchange/ppermute | solution.py:259
  64.4 0.0 collective-permute-done.2.refs_3_
  64.4 6.2 %collective-permute-done.1.refs_2_ = bf16[64,16,256]{2,1,0:T(8,128)(2,1)S(1)} collective-permute-done((bf16[64,16,256]{2,1,0:T(8,128)(2,1)}, bf16[64,16,256]{2,1,0:T(8,128)(2,1)S(1)}, u32[]{:S(2)}, u32[]{:S(2)}) %collective-permute-start.1) | collective-permute-done | bytes 524320 | tf_op jit(solution)/shard_map/kernel_exchange/ppermute | solution.py:259
  70.7 0.8 copy-done.8
  71.5 0.0 collective-permute-done.refs_1_
  71.5 0.0 all-to-all-done
  71.5 5.6 %shard_map.74 = bf16[256,128]{1,0:T(8,128)(2,1)S(1)} custom-call(s32[1]{0:T(128)} %bitcast.me_ref, bf16[2048,128]{1,0:T(8,128)(2,1)S(1)} %bitcast.51, bf16[512,1024]{1,0:T(8,128)(2,1)} %constant.55.clone.fwd_ref, bf16[1024,512]{1,0:T(8,128)(2,1)} %constant.56.clone.inv_ref, bf16[64,16,256]{2,1,0:T(8,128)(2,1)S(1)} %get-tuple-element.12.refs_0_, ...), custom_call_target="tpu_custom_call" | custom-call | flops 1000000000 | bytes 6815748 | tf_op jit(solution)/shard_map/pallas_call | solution.py:228
  77.1 13.7 %all_to_all.66 = bf16[32,8,128]{2,1,0:T(8,128)(2,1)S(1)} all-to-all(bf16[32,8,128]{2,1,0:T(8,128)(2,1)S(1)} %bitcast.59), channel_id=1, replica_groups=mesh['xl'=2,'zh'=4,'zl'=2,'yh'=2,'yl'=2,'xh'=2,'c'=2] {'xh','c','xl','zl..., dimensions={0} | all-to-all | bytes 131072 | tf_op jit(solution)/shard_map/to_rows/all_to_all | solution.py:285
  90.8 0.4 shard_map.75
  91.2 32.5 %all_to_all.67 = bf16[256,8,128]{2,1,0:T(8,128)(2,1)S(1)} all-to-all(bf16[256,8,128]{2,1,0:T(8,128)(2,1)S(1)} %bitcast.49), channel_id=1, replica_groups=mesh['xl'=2,'zh'=4,'zl'=2,'yh'=2,'yl'=2,'xh'=2,'c'=2] {'xh','c','xl','zh..., dimensions={0} | all-to-all | bytes 1048576 | tf_op jit(solution)/shard_map/to_wavenumbers/all_to_all | solution.py:267
  123.8 5.5 %shard_map.76 = bf16[256,128]{1,0:T(8,128)(2,1)S(1)} custom-call(s32[1]{0:T(128)} %bitcast.me_ref, bf16[2048,128]{1,0:T(8,128)(2,1)S(1)} %bitcast.53, bf16[512,1024]{1,0:T(8,128)(2,1)} %constant.55.clone.fwd_ref, bf16[1024,512]{1,0:T(8,128)(2,1)} %constant.56.clone.inv_ref, bf16[64,16,256]{2,1,0:T(8,128)(2,1)S(1)} %get-tuple-element.12.refs_0_, ...), custom_call_target="tpu_custom_call" | custom-call | flops 1000000000 | bytes 6815748 | tf_op jit(solution)/shard_map/pallas_call | solution.py:228
  129.3 10.6 %all_to_all.68 = bf16[32,8,128]{2,1,0:T(8,128)(2,1)S(1)} all-to-all(bf16[32,8,128]{2,1,0:T(8,128)(2,1)S(1)} %bitcast.60), channel_id=1, replica_groups=mesh['xl'=2,'zh'=4,'zl'=2,'yh'=2,'yl'=2,'xh'=2,'c'=2] {'xh','c','xl','zl..., dimensions={0} | all-to-all | bytes 131072 | tf_op jit(solution)/shard_map/to_rows/all_to_all | solution.py:285
  140.0 0.4 shard_map.77
  140.4 26.2 %all_to_all.69 = bf16[256,8,128]{2,1,0:T(8,128)(2,1)S(1)} all-to-all(bf16[256,8,128]{2,1,0:T(8,128)(2,1)S(1)} %bitcast.50), channel_id=1, replica_groups=mesh['xl'=2,'zh'=4,'zl'=2,'yh'=2,'yl'=2,'xh'=2,'c'=2] {'xh','c','xl','zh..., dimensions={0} | all-to-all | bytes 1048576 | tf_op jit(solution)/shard_map/to_wavenumbers/all_to_all | solution.py:267
  166.6 5.5 %shard_map.78 = bf16[256,128]{1,0:T(8,128)(2,1)S(1)} custom-call(s32[1]{0:T(128)} %bitcast.me_ref, bf16[2048,128]{1,0:T(8,128)(2,1)S(1)} %bitcast.52, bf16[512,1024]{1,0:T(8,128)(2,1)} %constant.55.clone.fwd_ref, bf16[1024,512]{1,0:T(8,128)(2,1)} %constant.56.clone.inv_ref, bf16[64,16,256]{2,1,0:T(8,128)(2,1)S(1)} %get-tuple-element.12.refs_0_, ...), custom_call_target="tpu_custom_call" | custom-call | flops 1000000000 | bytes 6815748 | tf_op jit(solution)/shard_map/pallas_call | solution.py:228
  172.2 10.6 %all_to_all.70 = bf16[32,8,128]{2,1,0:T(8,128)(2,1)S(1)} all-to-all(bf16[32,8,128]{2,1,0:T(8,128)(2,1)S(1)} %bitcast.58), channel_id=1, replica_groups=mesh['xl'=2,'zh'=4,'zl'=2,'yh'=2,'yl'=2,'xh'=2,'c'=2] {'xh','c','xl','zl..., dimensions={0} | all-to-all | bytes 131072 | tf_op jit(solution)/shard_map/to_rows/all_to_all | solution.py:285
  182.8 0.8 shard_map.79
  (15 shorter events, 0.0 us)
Async XLA Ops:
  0.0 8.5 %copy-start = (bf16[256,256]{1,0:T(8,128)(2,1)S(1)}, bf16[256,256]{1,0:T(8,128)(2,1)}, u32[]{:S(2)}) copy-start(bf16[256,256]{1,0:T(8,128)(2,1)} %constant.54.clone.table_ref.inv_ref) | copy-start | bytes 393220
  0.0 8.5 %copy-start.1 = (f32[1,2,2,32,128]{4,3,2,1,0:T(8,128)S(1)}, f32[1,2,2,32,128]{4,3,2,1,0:T(8,128)}, u32[]{:S(2)}) copy-start(f32[1,2,2,32,128]{4,3,2,1,0:T(8,128)} %param.7) | copy-start | bytes 196612
  0.0 8.5 %copy-start.2 = (f32[1,32,128]{2,1,0:T(8,128)S(1)}, f32[1,32,128]{2,1,0:T(8,128)}, u32[]{:S(2)}) copy-start(f32[1,32,128]{2,1,0:T(8,128)} %param.8) | copy-start | bytes 49156
  4.1 24.3 %collective-permute-start.6 = (bf16[64,16,256]{2,1,0:T(8,128)(2,1)}, bf16[64,16,256]{2,1,0:T(8,128)(2,1)S(1)}, u32[]{:S(2)}, u32[]{:S(2)}) collective-permute-start(bf16[64,16,256]{2,1,0:T(8,128)(2,1)} %get-tuple-element.5), channel_id=1, source_target_pairs={{0,148},{4,144},{16,132},{20,128},{128,20},{132,16},{144,4},{148,0... | collective-permute-start | bytes 1572872 | tf_op jit(solution)/shard_map/kernel_exchange/ppermute | solution.py:259
  8.5 25.7 %collective-permute-start.5 = (bf16[64,16,256]{2,1,0:T(8,128)(2,1)S(1)}, bf16[64,16,256]{2,1,0:T(8,128)(2,1)S(1)}, u32[]{:S(2)}, u32[]{:S(2)}) collective-permute-start(bf16[64,16,256]{2,1,0:T(8,128)(2,1)S(1)} %get-tuple-element.6), channel_id=1, source_target_pairs={{0,144},{4,148},{16,128},{20,132},{128,16},{132,20},{144,0},{148,4... | collective-permute-start | bytes 1572872 | tf_op jit(solution)/shard_map/kernel_exchange/ppermute | solution.py:259
  9.5 62.0 %all-to-all-start = ((bf16[256,8,128]{2,1,0:T(8,128)(2,1)}), bf16[256,8,128]{2,1,0:T(8,128)(2,1)S(1)}, u32[]{:S(2)}, u32[]{:S(2)}) async-start(bf16[256,8,128]{2,1,0:T(8,128)(2,1)} %bitcast.3), calls=%async_computation | async-start | bytes 1048576 | tf_op jit(solution)/shard_map/to_wavenumbers/all_to_all | solution.py:267
  24.4 29.6 %collective-permute-start.4 = (bf16[64,16,256]{2,1,0:T(8,128)(2,1)}, bf16[64,16,256]{2,1,0:T(8,128)(2,1)S(1)}, u32[]{:S(2)}, u32[]{:S(2)}) collective-permute-start(bf16[64,16,256]{2,1,0:T(8,128)(2,1)} %get-tuple-element.7), channel_id=1, source_target_pairs={{0,132},{4,128},{16,148},{20,144},{128,4},{132,0},{144,20},{148,16... | collective-permute-start | bytes 1572872 | tf_op jit(solution)/shard_map/kernel_exchange/ppermute | solution.py:259
  26.8 37.7 %collective-permute-start.3 = (bf16[64,16,256]{2,1,0:T(8,128)(2,1)}, bf16[64,16,256]{2,1,0:T(8,128)(2,1)S(1)}, u32[]{:S(2)}, u32[]{:S(2)}) collective-permute-start(bf16[64,16,256]{2,1,0:T(8,128)(2,1)} %get-tuple-element.8), channel_id=1, source_target_pairs={{0,128},{4,132},{16,144},{20,148},{128,0},{132,4},{144,16},{148,20... | collective-permute-start | bytes 1572872 | tf_op jit(solution)/shard_map/kernel_exchange/ppermute | solution.py:259
  27.0 37.4 %collective-permute-start.2 = (bf16[64,16,256]{2,1,0:T(8,128)(2,1)}, bf16[64,16,256]{2,1,0:T(8,128)(2,1)S(1)}, u32[]{:S(2)}, u32[]{:S(2)}) collective-permute-start(bf16[64,16,256]{2,1,0:T(8,128)(2,1)} %get-tuple-element.9), channel_id=1, source_target_pairs={{0,20},{4,16},{16,4},{20,0},{128,148},{132,144},{144,132},{148,128... | collective-permute-start | bytes 1572872 | tf_op jit(solution)/shard_map/kernel_exchange/ppermute | solution.py:259
  28.3 43.2 %copy-start.3 = (bf16[64,16,256]{2,1,0:T(8,128)(2,1)}, bf16[64,16,256]{2,1,0:T(8,128)(2,1)S(1)}, u32[]{:S(2)}) copy-start(bf16[64,16,256]{2,1,0:T(8,128)(2,1)S(1)} %collective-permute-done.6.refs_7_) | copy-start | bytes 1572868
  28.3 42.3 %collective-permute-start.1 = (bf16[64,16,256]{2,1,0:T(8,128)(2,1)}, bf16[64,16,256]{2,1,0:T(8,128)(2,1)S(1)}, u32[]{:S(2)}, u32[]{:S(2)}) collective-permute-start(bf16[64,16,256]{2,1,0:T(8,128)(2,1)} %get-tuple-element.10), channel_id=1, source_target_pairs={{0,16},{4,20},{16,0},{20,4},{128,144},{132,148},{144,128},{148,132... | collective-permute-start | bytes 1572872 | tf_op jit(solution)/shard_map/kernel_exchange/ppermute | solution.py:259
  34.2 37.3 %copy-start.4 = (bf16[64,16,256]{2,1,0:T(8,128)(2,1)}, bf16[64,16,256]{2,1,0:T(8,128)(2,1)S(1)}, u32[]{:S(2)}) copy-start(bf16[64,16,256]{2,1,0:T(8,128)(2,1)S(1)} %collective-permute-done.5.refs_6_) | copy-start | bytes 1572868
  34.2 37.3 %collective-permute-start = (bf16[64,16,256]{2,1,0:T(8,128)(2,1)}, bf16[64,16,256]{2,1,0:T(8,128)(2,1)S(1)}, u32[]{:S(2)}, u32[]{:S(2)}) collective-permute-start(bf16[64,16,256]{2,1,0:T(8,128)(2,1)} %get-tuple-element.11), channel_id=1, source_target_pairs={{0,4},{4,0},{16,20},{20,16},{128,132},{132,128},{144,148},{148,144... | collective-permute-start | bytes 1572872 | tf_op jit(solution)/shard_map/kernel_exchange/ppermute | solution.py:259
  54.0 17.5 %copy-start.5 = (bf16[64,16,256]{2,1,0:T(8,128)(2,1)}, bf16[64,16,256]{2,1,0:T(8,128)(2,1)S(1)}, u32[]{:S(2)}) copy-start(bf16[64,16,256]{2,1,0:T(8,128)(2,1)S(1)} %collective-permute-done.4.refs_5_) | copy-start | bytes 1572868
  64.4 6.2 %copy-start.6 = (bf16[64,16,256]{2,1,0:T(8,128)(2,1)}, bf16[64,16,256]{2,1,0:T(8,128)(2,1)S(1)}, u32[]{:S(2)}) copy-start(bf16[64,16,256]{2,1,0:T(8,128)(2,1)S(1)} %collective-permute-done.3.refs_4_) | copy-start | bytes 1572868
  64.4 6.2 %copy-start.7 = (bf16[64,16,256]{2,1,0:T(8,128)(2,1)}, bf16[64,16,256]{2,1,0:T(8,128)(2,1)S(1)}, u32[]{:S(2)}) copy-start(bf16[64,16,256]{2,1,0:T(8,128)(2,1)S(1)} %collective-permute-done.2.refs_3_) | copy-start | bytes 1572868
  70.7 0.8 copy-start.8

commit v3 on v2

--- a/solution.py
+++ b/solution.py
@@ -124,7 +124,7 @@
             out_ref[s, part] = parts[part]
 
 
-SENT = (1, 2, 3, 4, 5, 6, 7)
+CUT_GROUPS = ((6, 7), (0, 1, 2, 3, 4, 5))
 COUPLE_MIB = 52
 BLOCK = 2
 
@@ -182,7 +182,7 @@
             return tuple(out)
 
         zero = jnp.zeros((KYS, P_SIZE), jnp.float32)
-        sums = lax.fori_loop(0, NZ, step, (zero,) * (len(block) * SRC * 2), unroll=4)
+        sums = lax.fori_loop(0, NZ, step, (zero,) * (len(block) * SRC * 2), unroll=8)
         for j, n in enumerate(block):
             for quarter in range(2 * SRC):
                 put(n, quarter, sums[j * 2 * SRC + quarter])
@@ -252,11 +252,17 @@
     kern = kernel[0].reshape(NZ, 2, SHARES, KYS, P_SIZE)
 
     with jax.named_scope("kernel_exchange"):
-        slabs = [None] * SHARES
-        for offset in (0,) + SENT:
-            piece = lax.dynamic_index_in_dim(kern, me[0] ^ offset, axis=2, keepdims=False)
-            piece = piece.reshape(NZ, 2 * KYS, P_SIZE)
-            slabs[offset] = lax.ppermute(piece, SHARE, swap_perm(offset)) if offset else piece
+        pieces = {}
+        place = me[0]
+        for group in CUT_GROUPS:
+            for offset in group:
+                piece = lax.dynamic_index_in_dim(kern, place ^ offset, axis=2, keepdims=False)
+                pieces[offset] = piece.reshape(NZ, 2 * KYS, P_SIZE)
+            first = group[0]
+            pieces[first], place = lax.optimization_barrier((pieces[first], place))
+        slabs = [pieces[0]]
+        for offset in range(1, SHARES):
+            slabs.append(lax.ppermute(pieces[offset], SHARE, swap_perm(offset)))
 
     send_shape = jax.ShapeDtypeStruct((ALL_ROWS, LANES), jnp.bfloat16)
     back_shape = jax.ShapeDtypeStruct((LATS * SHARES * KYS, LANES), jnp.bfloat16)

time: 184 us -> 181 us (0.984)
  waiting for transfers between devices: 42.2 us -> 37.8 us
    ppermute x7, waiting for transfers between devices: 42.2 us -> 37.8 us  [local(): slabs.append(lax.ppermute(pieces[offset], SHARE, swap_perm(offset)))]
    reshape x1 -> x2, local copies, waits for them, and re-layouts: 4.05 us -> 5.49 us  [local(): pieces[offset] = piece.reshape(NZ, 2 * KYS, P_SIZE)]
  transfers between devices with their start and end apart: 8 -> 8, of which waited for: 4 -> 4; matrix products, arithmetic and copies ran while one was open for 0% -> 2% of each run, Pallas kernels for 1% -> 1%
where the time goes in v3:
time: 181 us
  blocking collectives  93.4 us (52%)
  waiting for transfers between devices  37.8 us (21%)
  starting transfers between devices  24.6 us (14%)
  Pallas kernels  18.7 us (10%)
  local copies, waits for them, and re-layouts  6.34 us (4%)
    all_to_all x2, blocking collectives, local(): got = lax.all_to_all(sent, LAT + DEPTH, 0, 0, tiled=True)  58.9 us
    ppermute x7, waiting for transfers between devices, local(): slabs.append(lax.ppermute(pieces[offset], SHARE, swap_perm(offset)))  37.8 us
    all_to_all x3, blocking collectives, local(): rows = lax.all_to_all(back, LAT + SHARE, 0, 0, tiled=True)  34.5 us
    pallas_call x7, Pallas kernels, call(): pl.pallas_call(body, out_shape=out, in_specs=specs or [VMEM] * len(args),...  18.7 us
    all_to_all x1, starting transfers between devices, local(): got = lax.all_to_all(sent, LAT + DEPTH, 0, 0, tiled=True)  14.9 us
    ppermute x7, starting transfers between devices, local(): slabs.append(lax.ppermute(pieces[offset], SHARE, swap_perm(offset)))  9.73 us
    reshape x2, local copies, waits for them, and re-layouts, local(): pieces[offset] = piece.reshape(NZ, 2 * KYS, P_SIZE)  5.49 us
  transfers between devices with their start and end apart: 8, of which 4 were waited for; matrix products, arithmetic and copies ran while one was open for 2% of the time, Pallas kernels for 1%

profile of v3, /device:TPU:1, one launch (start us, length us, event | category | flops | bytes accessed | tf_op | source)
XLA Modules:
  0.0 181.0 jit_solution(1685943777109850852)
XLA Ops:
  0.0 1.9 %dynamic-slice_bitcast_fusion.7 = bf16[64,16,256]{2,1,0:T(8,128)(2,1)} fusion(bf16[64,2,8,8,256]{4,3,2,1,0:T(8,128)(2,1)} %bitcast.67, s32[]{:T(128)S(6)} %select_n.25), kind=kLoop, calls=%fused_computation.7 | loop fusion | bytes 1048580 | tf_op jit(solution)/shard_map/kernel_exchange/reshape | solution.py:260
  1.9 3.4 %collective-permute-start.5 = (bf16[64,16,256]{2,1,0:T(8,128)(2,1)}, bf16[64,16,256]{2,1,0:T(8,128)(2,1)S(1)}, u32[]{:S(2)}, u32[]{:S(2)}) collective-permute-start(bf16[64,16,256]{2,1,0:T(8,128)(2,1)} %dynamic-slice_bitcast_fusion.7), channel_id=1, source_target_pairs={{0,144},{4,148},{16,128},{20,132},{128,16},{132,20},{144,0},{148,4... | collective-permute-start | bytes 1572872 | tf_op jit(solution)/shard_map/kernel_exchange/ppermute | solution.py:265
  5.3 3.6 %dynamic-slice_bitcast_fusion = (bf16[64,16,256]{2,1,0:T(8,128)(2,1)S(1)}, bf16[64,16,256]{2,1,0:T(8,128)(2,1)}, bf16[64,16,256]{2,1,0:T(8,128)(2,1)}, bf16[64,1...) fusion(bf16[64,2,8,8,256]{4,3,2,1,0:T(8,128)(2,1)} %bitcast.68,, ...), kind=kLoop, calls=%fused_computation | loop fusion | bytes 7340060 | tf_op jit(solution)/shard_map/kernel_exchange/reshape | solution.py:260
  8.9 1.0 collective-permute-start.6
  9.9 0.0 copy-done
  9.9 1.0 shard_map.73
  10.9 14.9 %all-to-all-start = ((bf16[256,8,128]{2,1,0:T(8,128)(2,1)}), bf16[256,8,128]{2,1,0:T(8,128)(2,1)S(1)}, u32[]{:S(2)}, u32[]{:S(2)}) async-start(bf16[256,8,128]{2,1,0:T(8,128)(2,1)} %bitcast.3), calls=%async_computation | async-start | bytes 1048576 | tf_op jit(solution)/shard_map/to_wavenumbers/all_to_all | solution.py:273
  25.8 2.4 %collective-permute-start.4 = (bf16[64,16,256]{2,1,0:T(8,128)(2,1)}, bf16[64,16,256]{2,1,0:T(8,128)(2,1)S(1)}, u32[]{:S(2)}, u32[]{:S(2)}) collective-permute-start(bf16[64,16,256]{2,1,0:T(8,128)(2,1)} %get-tuple-element.12), channel_id=1, source_target_pairs={{0,132},{4,128},{16,148},{20,144},{128,4},{132,0},{144,20},{148,16... | collective-permute-start | bytes 1572872 | tf_op jit(solution)/shard_map/kernel_exchange/ppermute | solution.py:265
  28.2 0.3 collective-permute-start.3
  28.5 1.3 collective-permute-start.2
  29.8 0.0 collective-permute-done.5.refs_6_
  29.8 0.2 collective-permute-start.1
  29.9 0.0 collective-permute-done.6.refs_7_
  30.0 1.2 collective-permute-start
  31.2 20.1 %collective-permute-done.4.refs_5_ = bf16[64,16,256]{2,1,0:T(8,128)(2,1)S(1)} collective-permute-done((bf16[64,16,256]{2,1,0:T(8,128)(2,1)}, bf16[64,16,256]{2,1,0:T(8,128)(2,1)S(1)}, u32[]{:S(2)}, u32[]{:S(2)}) %collective-permute-start.4) | collective-permute-done | bytes 524320 | tf_op jit(solution)/shard_map/kernel_exchange/ppermute | solution.py:265
  51.3 11.4 %collective-permute-done.3.refs_4_ = bf16[64,16,256]{2,1,0:T(8,128)(2,1)S(1)} collective-permute-done((bf16[64,16,256]{2,1,0:T(8,128)(2,1)}, bf16[64,16,256]{2,1,0:T(8,128)(2,1)S(1)}, u32[]{:S(2)}, u32[]{:S(2)}) %collective-permute-start.3) | collective-permute-done | bytes 524320 | tf_op jit(solution)/shard_map/kernel_exchange/ppermute | solution.py:265
  62.6 0.0 collective-permute-done.2.refs_3_
  62.6 5.5 %collective-permute-done.1.refs_2_ = bf16[64,16,256]{2,1,0:T(8,128)(2,1)S(1)} collective-permute-done((bf16[64,16,256]{2,1,0:T(8,128)(2,1)}, bf16[64,16,256]{2,1,0:T(8,128)(2,1)S(1)}, u32[]{:S(2)}, u32[]{:S(2)}) %collective-permute-start.1) | collective-permute-done | bytes 524320 | tf_op jit(solution)/shard_map/kernel_exchange/ppermute | solution.py:265
  68.2 0.8 copy-done.8
  69.0 0.8 collective-permute-done.refs_1_
  69.8 0.0 all-to-all-done
  69.8 5.4 %shard_map.74 = bf16[256,128]{1,0:T(8,128)(2,1)S(1)} custom-call(s32[1]{0:T(128)} %bitcast.me_ref, bf16[2048,128]{1,0:T(8,128)(2,1)S(1)} %bitcast.51, bf16[512,1024]{1,0:T(8,128)(2,1)} %constant.55.clone.fwd_ref, bf16[1024,512]{1,0:T(8,128)(2,1)} %constant.56.clone.inv_ref, bf16[64,16,256]{2,1,0:T(8,128)(2,1)S(1)} %get-tuple-element.9.refs_0_, ...), custom_call_target="tpu_custom_call" | custom-call | flops 1000000000 | bytes 6815748 | tf_op jit(solution)/shard_map/pallas_call | solution.py:228
  75.2 13.2 %all_to_all.66 = bf16[32,8,128]{2,1,0:T(8,128)(2,1)S(1)} all-to-all(bf16[32,8,128]{2,1,0:T(8,128)(2,1)S(1)} %bitcast.59), channel_id=1, replica_groups=mesh['xl'=2,'zh'=4,'zl'=2,'yh'=2,'yl'=2,'xh'=2,'c'=2] {'xh','c','xl','zl..., dimensions={0} | all-to-all | bytes 131072 | tf_op jit(solution)/shard_map/to_rows/all_to_all | solution.py:291
  88.4 0.4 shard_map.75
  88.8 32.5 %all_to_all.67 = bf16[256,8,128]{2,1,0:T(8,128)(2,1)S(1)} all-to-all(bf16[256,8,128]{2,1,0:T(8,128)(2,1)S(1)} %bitcast.49), channel_id=1, replica_groups=mesh['xl'=2,'zh'=4,'zl'=2,'yh'=2,'yl'=2,'xh'=2,'c'=2] {'xh','c','xl','zh..., dimensions={0} | all-to-all | bytes 1048576 | tf_op jit(solution)/shard_map/to_wavenumbers/all_to_all | solution.py:273
  121.2 5.4 %shard_map.76 = bf16[256,128]{1,0:T(8,128)(2,1)S(1)} custom-call(s32[1]{0:T(128)} %bitcast.me_ref, bf16[2048,128]{1,0:T(8,128)(2,1)S(1)} %bitcast.53, bf16[512,1024]{1,0:T(8,128)(2,1)} %constant.55.clone.fwd_ref, bf16[1024,512]{1,0:T(8,128)(2,1)} %constant.56.clone.inv_ref, bf16[64,16,256]{2,1,0:T(8,128)(2,1)S(1)} %get-tuple-element.9.refs_0_, ...), custom_call_target="tpu_custom_call" | custom-call | flops 1000000000 | bytes 6815748 | tf_op jit(solution)/shard_map/pallas_call | solution.py:228
  126.6 10.6 %all_to_all.68 = bf16[32,8,128]{2,1,0:T(8,128)(2,1)S(1)} all-to-all(bf16[32,8,128]{2,1,0:T(8,128)(2,1)S(1)} %bitcast.60), channel_id=1, replica_groups=mesh['xl'=2,'zh'=4,'zl'=2,'yh'=2,'yl'=2,'xh'=2,'c'=2] {'xh','c','xl','zl..., dimensions={0} | all-to-all | bytes 131072 | tf_op jit(solution)/shard_map/to_rows/all_to_all | solution.py:291
  137.3 0.4 shard_map.77
  137.7 26.4 %all_to_all.69 = bf16[256,8,128]{2,1,0:T(8,128)(2,1)S(1)} all-to-all(bf16[256,8,128]{2,1,0:T(8,128)(2,1)S(1)} %bitcast.50), channel_id=1, replica_groups=mesh['xl'=2,'zh'=4,'zl'=2,'yh'=2,'yl'=2,'xh'=2,'c'=2] {'xh','c','xl','zh..., dimensions={0} | all-to-all | bytes 1048576 | tf_op jit(solution)/shard_map/to_wavenumbers/all_to_all | solution.py:273
  164.1 5.4 %shard_map.78 = bf16[256,128]{1,0:T(8,128)(2,1)S(1)} custom-call(s32[1]{0:T(128)} %bitcast.me_ref, bf16[2048,128]{1,0:T(8,128)(2,1)S(1)} %bitcast.52, bf16[512,1024]{1,0:T(8,128)(2,1)} %constant.55.clone.fwd_ref, bf16[1024,512]{1,0:T(8,128)(2,1)} %constant.56.clone.inv_ref, bf16[64,16,256]{2,1,0:T(8,128)(2,1)S(1)} %get-tuple-element.9.refs_0_, ...), custom_call_target="tpu_custom_call" | custom-call | flops 1000000000 | bytes 6815748 | tf_op jit(solution)/shard_map/pallas_call | solution.py:228
  169.5 10.7 %all_to_all.70 = bf16[32,8,128]{2,1,0:T(8,128)(2,1)S(1)} all-to-all(bf16[32,8,128]{2,1,0:T(8,128)(2,1)S(1)} %bitcast.58), channel_id=1, replica_groups=mesh['xl'=2,'zh'=4,'zl'=2,'yh'=2,'yl'=2,'xh'=2,'c'=2] {'xh','c','xl','zl..., dimensions={0} | all-to-all | bytes 131072 | tf_op jit(solution)/shard_map/to_rows/all_to_all | solution.py:291
  180.1 0.8 shard_map.79
  (16 shorter events, 0.0 us)
Async XLA Ops:
  0.0 9.9 %copy-start = (bf16[256,256]{1,0:T(8,128)(2,1)S(1)}, bf16[256,256]{1,0:T(8,128)(2,1)}, u32[]{:S(2)}) copy-start(bf16[256,256]{1,0:T(8,128)(2,1)} %constant.54.clone.table_ref.inv_ref) | copy-start | bytes 393220
  0.0 9.9 %copy-start.1 = (f32[1,2,2,32,128]{4,3,2,1,0:T(8,128)S(1)}, f32[1,2,2,32,128]{4,3,2,1,0:T(8,128)}, u32[]{:S(2)}) copy-start(f32[1,2,2,32,128]{4,3,2,1,0:T(8,128)} %param.7) | copy-start | bytes 196612
  0.0 9.9 %copy-start.2 = (f32[1,32,128]{2,1,0:T(8,128)S(1)}, f32[1,32,128]{2,1,0:T(8,128)}, u32[]{:S(2)}) copy-start(f32[1,32,128]{2,1,0:T(8,128)} %param.8) | copy-start | bytes 49156
  1.9 27.8 %collective-permute-start.5 = (bf16[64,16,256]{2,1,0:T(8,128)(2,1)}, bf16[64,16,256]{2,1,0:T(8,128)(2,1)S(1)}, u32[]{:S(2)}, u32[]{:S(2)}) collective-permute-start(bf16[64,16,256]{2,1,0:T(8,128)(2,1)} %dynamic-slice_bitcast_fusion.7), channel_id=1, source_target_pairs={{0,144},{4,148},{16,128},{20,132},{128,16},{132,20},{144,0},{148,4... | collective-permute-start | bytes 1572872 | tf_op jit(solution)/shard_map/kernel_exchange/ppermute | solution.py:265
  8.9 21.1 %collective-permute-start.6 = (bf16[64,16,256]{2,1,0:T(8,128)(2,1)S(1)}, bf16[64,16,256]{2,1,0:T(8,128)(2,1)S(1)}, u32[]{:S(2)}, u32[]{:S(2)}) collective-permute-start(bf16[64,16,256]{2,1,0:T(8,128)(2,1)S(1)} %get-tuple-element.11), channel_id=1, source_target_pairs={{0,148},{4,144},{16,132},{20,128},{128,20},{132,16},{144,4},{148,0... | collective-permute-start | bytes 1572872 | tf_op jit(solution)/shard_map/kernel_exchange/ppermute | solution.py:265
  10.9 58.8 %all-to-all-start = ((bf16[256,8,128]{2,1,0:T(8,128)(2,1)}), bf16[256,8,128]{2,1,0:T(8,128)(2,1)S(1)}, u32[]{:S(2)}, u32[]{:S(2)}) async-start(bf16[256,8,128]{2,1,0:T(8,128)(2,1)} %bitcast.3), calls=%async_computation | async-start | bytes 1048576 | tf_op jit(solution)/shard_map/to_wavenumbers/all_to_all | solution.py:273
  25.8 25.4 %collective-permute-start.4 = (bf16[64,16,256]{2,1,0:T(8,128)(2,1)}, bf16[64,16,256]{2,1,0:T(8,128)(2,1)S(1)}, u32[]{:S(2)}, u32[]{:S(2)}) collective-permute-start(bf16[64,16,256]{2,1,0:T(8,128)(2,1)} %get-tuple-element.12), channel_id=1, source_target_pairs={{0,132},{4,128},{16,148},{20,144},{128,4},{132,0},{144,20},{148,16... | collective-permute-start | bytes 1572872 | tf_op jit(solution)/shard_map/kernel_exchange/ppermute | solution.py:265
  28.2 34.4 %collective-permute-start.3 = (bf16[64,16,256]{2,1,0:T(8,128)(2,1)}, bf16[64,16,256]{2,1,0:T(8,128)(2,1)S(1)}, u32[]{:S(2)}, u32[]{:S(2)}) collective-permute-start(bf16[64,16,256]{2,1,0:T(8,128)(2,1)} %get-tuple-element.13), channel_id=1, source_target_pairs={{0,128},{4,132},{16,144},{20,148},{128,0},{132,4},{144,16},{148,20... | collective-permute-start | bytes 1572872 | tf_op jit(solution)/shard_map/kernel_exchange/ppermute | solution.py:265
  28.5 34.2 %collective-permute-start.2 = (bf16[64,16,256]{2,1,0:T(8,128)(2,1)}, bf16[64,16,256]{2,1,0:T(8,128)(2,1)S(1)}, u32[]{:S(2)}, u32[]{:S(2)}) collective-permute-start(bf16[64,16,256]{2,1,0:T(8,128)(2,1)} %get-tuple-element.14), channel_id=1, source_target_pairs={{0,20},{4,16},{16,4},{20,0},{128,148},{132,144},{144,132},{148,128... | collective-permute-start | bytes 1572872 | tf_op jit(solution)/shard_map/kernel_exchange/ppermute | solution.py:265
  29.8 40.0 %copy-start.3 = (bf16[64,16,256]{2,1,0:T(8,128)(2,1)}, bf16[64,16,256]{2,1,0:T(8,128)(2,1)S(1)}, u32[]{:S(2)}) copy-start(bf16[64,16,256]{2,1,0:T(8,128)(2,1)S(1)} %collective-permute-done.5.refs_6_) | copy-start | bytes 1572868
  29.8 38.4 %collective-permute-start.1 = (bf16[64,16,256]{2,1,0:T(8,128)(2,1)}, bf16[64,16,256]{2,1,0:T(8,128)(2,1)S(1)}, u32[]{:S(2)}, u32[]{:S(2)}) collective-permute-start(bf16[64,16,256]{2,1,0:T(8,128)(2,1)} %get-tuple-element.15), channel_id=1, source_target_pairs={{0,16},{4,20},{16,0},{20,4},{128,144},{132,148},{144,128},{148,132... | collective-permute-start | bytes 1572872 | tf_op jit(solution)/shard_map/kernel_exchange/ppermute | solution.py:265
  30.0 39.8 %copy-start.4 = (bf16[64,16,256]{2,1,0:T(8,128)(2,1)}, bf16[64,16,256]{2,1,0:T(8,128)(2,1)S(1)}, u32[]{:S(2)}) copy-start(bf16[64,16,256]{2,1,0:T(8,128)(2,1)S(1)} %collective-permute-done.6.refs_7_) | copy-start | bytes 1572868
  30.0 39.8 %collective-permute-start = (bf16[64,16,256]{2,1,0:T(8,128)(2,1)}, bf16[64,16,256]{2,1,0:T(8,128)(2,1)S(1)}, u32[]{:S(2)}, u32[]{:S(2)}) collective-permute-start(bf16[64,16,256]{2,1,0:T(8,128)(2,1)} %get-tuple-element.16), channel_id=1, source_target_pairs={{0,4},{4,0},{16,20},{20,16},{128,132},{132,128},{144,148},{148,144... | collective-permute-start | bytes 1572872 | tf_op jit(solution)/shard_map/kernel_exchange/ppermute | solution.py:265
  51.3 18.5 %copy-start.5 = (bf16[64,16,256]{2,1,0:T(8,128)(2,1)}, bf16[64,16,256]{2,1,0:T(8,128)(2,1)S(1)}, u32[]{:S(2)}) copy-start(bf16[64,16,256]{2,1,0:T(8,128)(2,1)S(1)} %collective-permute-done.4.refs_5_) | copy-start | bytes 1572868
  62.6 5.5 %copy-start.6 = (bf16[64,16,256]{2,1,0:T(8,128)(2,1)}, bf16[64,16,256]{2,1,0:T(8,128)(2,1)S(1)}, u32[]{:S(2)}) copy-start(bf16[64,16,256]{2,1,0:T(8,128)(2,1)S(1)} %collective-permute-done.3.refs_4_) | copy-start | bytes 1572868
  62.6 5.5 %copy-start.7 = (bf16[64,16,256]{2,1,0:T(8,128)(2,1)}, bf16[64,16,256]{2,1,0:T(8,128)(2,1)S(1)}, u32[]{:S(2)}) copy-start(bf16[64,16,256]{2,1,0:T(8,128)(2,1)S(1)} %collective-permute-done.2.refs_3_) | copy-start | bytes 1572868
  68.2 0.8 copy-start.8

commit v4 on v3

--- a/solution.py
+++ b/solution.py
@@ -90,7 +90,8 @@
         out_ref[dst : dst + pair, :] = along_y[src : src + pair, :]
 
 
-def first_body(incident_ref, contrast_ref, table_ref, out_ref):
+def first_body(incident_ref, contrast_ref, table_ref, cut_ref, out_ref):
+    del cut_ref
     parts = [(incident_ref[s, 0], incident_ref[s, 1]) for s in range(SRC)]
     send_sources(parts, contrast_ref, table_ref, out_ref)
 
@@ -124,7 +125,7 @@
             out_ref[s, part] = parts[part]
 
 
-CUT_GROUPS = ((6, 7), (0, 1, 2, 3, 4, 5))
+CUT_GROUPS = ((6,), (7,), (5, 4, 3, 2, 1, 0))
 COUPLE_MIB = 52
 BLOCK = 2
 
@@ -258,8 +259,8 @@
             for offset in group:
                 piece = lax.dynamic_index_in_dim(kern, place ^ offset, axis=2, keepdims=False)
                 pieces[offset] = piece.reshape(NZ, 2 * KYS, P_SIZE)
-            first = group[0]
-            pieces[first], place = lax.optimization_barrier((pieces[first], place))
+            cut, place = lax.optimization_barrier(([pieces[j] for j in group], place))
+            pieces.update(zip(group, cut))
         slabs = [pieces[0]]
         for offset in range(1, SHARES):
             slabs.append(lax.ppermute(pieces[offset], SHARE, swap_perm(offset)))
@@ -267,7 +268,13 @@
     send_shape = jax.ShapeDtypeStruct((ALL_ROWS, LANES), jnp.bfloat16)
     back_shape = jax.ShapeDtypeStruct((LATS * SHARES * KYS, LANES), jnp.bfloat16)
     field_shape = jax.ShapeDtypeStruct((SRC, 2, XS, L), jnp.float32)
-    sent = call(first_body, send_shape, (incident, contrast, fwd_y), flops=10**7)
+    sent = call(
+        first_body,
+        send_shape,
+        (incident, contrast, fwd_y, slabs[0]),
+        specs=[VMEM] * 3 + [HBM],
+        flops=10**7,
+    )
     for iteration in range(ITERS):
         with jax.named_scope("to_wavenumbers"):
             got = lax.all_to_all(sent, LAT + DEPTH, 0, 0, tiled=True)

time: 181 us -> 185 us (1.022)
  local copies, waits for them, and re-layouts: 6.34 us -> 8.86 us
    reshape x2 -> x3, local copies, waits for them, and re-layouts: 5.49 us -> 7.21 us  [local(): pieces[offset] = piece.reshape(NZ, 2 * KYS, P_SIZE)]
  transfers between devices with their start and end apart: 8 -> 8, of which waited for: 4 -> 3; matrix products, arithmetic and copies ran while one was open for 2% -> 2% of each run, Pallas kernels for 1% -> 1%
where the time goes in v4:
time: 185 us
  blocking collectives  93.4 us (50%)
  waiting for transfers between devices  38.8 us (21%)
  starting transfers between devices  24.6 us (13%)
  Pallas kernels  18.7 us (10%)
  local copies, waits for them, and re-layouts  8.86 us (5%)
    all_to_all x2, blocking collectives, local(): got = lax.all_to_all(sent, LAT + DEPTH, 0, 0, tiled=True)  58.8 us
    ppermute x7, waiting for transfers between devices, local(): slabs.append(lax.ppermute(pieces[offset], SHARE, swap_perm(offset)))  38.8 us
    all_to_all x3, blocking collectives, local(): rows = lax.all_to_all(back, LAT + SHARE, 0, 0, tiled=True)  34.7 us
    pallas_call x7, Pallas kernels, call(): pl.pallas_call(body, out_shape=out, in_specs=specs or [VMEM] * len(args),...  18.7 us
    all_to_all x1, starting transfers between devices, local(): got = lax.all_to_all(sent, LAT + DEPTH, 0, 0, tiled=True)  14.9 us
    ppermute x7, starting transfers between devices, local(): slabs.append(lax.ppermute(pieces[offset], SHARE, swap_perm(offset)))  9.71 us
    reshape x3, local copies, waits for them, and re-layouts, local(): pieces[offset] = piece.reshape(NZ, 2 * KYS, P_SIZE)  7.21 us
  transfers between devices with their start and end apart: 8, of which 3 were waited for; matrix products, arithmetic and copies ran while one was open for 2% of the time, Pallas kernels for 1%

profile of v4, /device:TPU:1, one launch (start us, length us, event | category | flops | bytes accessed | tf_op | source)
XLA Modules:
  0.0 184.5 jit_solution(11176565850704255080)
XLA Ops:
  0.0 1.9 %dynamic-slice_bitcast_fusion.7 = bf16[64,16,256]{2,1,0:T(8,128)(2,1)} fusion(bf16[64,2,8,8,256]{4,3,2,1,0:T(8,128)(2,1)} %bitcast.67, s32[]{:T(128)S(6)} %select_n.25), kind=kLoop, calls=%fused_computation.7 | loop fusion | bytes 1048580 | tf_op jit(solution)/shard_map/kernel_exchange/reshape | solution.py:261
  1.9 1.9 %dynamic-slice_bitcast_fusion.6 = bf16[64,16,256]{2,1,0:T(8,128)(2,1)} fusion(bf16[64,2,8,8,256]{4,3,2,1,0:T(8,128)(2,1)} %bitcast.68, s32[]{:T(128)S(6)} %select_n.26), kind=kLoop, calls=%fused_computation.6 | loop fusion | bytes 1048580 | tf_op jit(solution)/shard_map/kernel_exchange/reshape | solution.py:261
  3.8 4.4 %collective-permute-start.6 = (bf16[64,16,256]{2,1,0:T(8,128)(2,1)}, bf16[64,16,256]{2,1,0:T(8,128)(2,1)S(1)}, u32[]{:S(2)}, u32[]{:S(2)}) collective-permute-start(bf16[64,16,256]{2,1,0:T(8,128)(2,1)} %dynamic-slice_bitcast_fusion.6), channel_id=1, source_target_pairs={{0,148},{4,144},{16,132},{20,128},{128,20},{132,16},{144,4},{148,0... | collective-permute-start | bytes 1572872 | tf_op jit(solution)/shard_map/kernel_exchange/ppermute | solution.py:266
  8.2 0.0 collective-permute-start.5
  8.2 3.4 %dynamic-slice_bitcast_fusion = (bf16[64,16,256]{2,1,0:T(8,128)(2,1)S(1)}, bf16[64,16,256]{2,1,0:T(8,128)(2,1)}, bf16[64,16,256]{2,1,0:T(8,128)(2,1)}, bf16[64,1...) fusion(bf16[64,2,8,8,256]{4,3,2,1,0:T(8,128)(2,1)} %bitcast.69, s32[]{:T(128)S(6)} %select_n.32, ...), kind=kLoop, calls=%fused_computation | loop fusion | bytes 6291480 | tf_op jit(solution)/shard_map/kernel_exchange/reshape | solution.py:261
  11.6 1.0 shard_map.73
  12.6 14.9 %all-to-all-start = ((bf16[256,8,128]{2,1,0:T(8,128)(2,1)}), bf16[256,8,128]{2,1,0:T(8,128)(2,1)S(1)}, u32[]{:S(2)}, u32[]{:S(2)}) async-start(bf16[256,8,128]{2,1,0:T(8,128)(2,1)} %bitcast.12), calls=%async_computation | async-start | bytes 1048576 | tf_op jit(solution)/shard_map/to_wavenumbers/all_to_all | solution.py:280
  27.6 1.5 collective-permute-start
  29.0 1.4 collective-permute-start.1
  30.4 0.0 collective-permute-start.2
  30.4 0.0 collective-permute-done.6.refs_7_
  30.4 1.3 collective-permute-start.3
  31.7 0.0 collective-permute-done.5.refs_6_
  31.7 1.2 collective-permute-start.4
  32.9 12.0 %collective-permute-done.refs_1_ = bf16[64,16,256]{2,1,0:T(8,128)(2,1)S(1)} collective-permute-done((bf16[64,16,256]{2,1,0:T(8,128)(2,1)}, bf16[64,16,256]{2,1,0:T(8,128)(2,1)S(1)}, u32[]{:S(2)}, u32[]{:S(2)}) %collective-permute-start) | collective-permute-done | bytes 524320 | tf_op jit(solution)/shard_map/kernel_exchange/ppermute | solution.py:266
  44.9 8.6 %collective-permute-done.1.refs_2_ = bf16[64,16,256]{2,1,0:T(8,128)(2,1)S(1)} collective-permute-done((bf16[64,16,256]{2,1,0:T(8,128)(2,1)}, bf16[64,16,256]{2,1,0:T(8,128)(2,1)S(1)}, u32[]{:S(2)}, u32[]{:S(2)}) %collective-permute-start.1) | collective-permute-done | bytes 524320 | tf_op jit(solution)/shard_map/kernel_exchange/ppermute | solution.py:266
  53.5 18.2 %collective-permute-done.2.refs_3_ = bf16[64,16,256]{2,1,0:T(8,128)(2,1)S(1)} collective-permute-done((bf16[64,16,256]{2,1,0:T(8,128)(2,1)}, bf16[64,16,256]{2,1,0:T(8,128)(2,1)S(1)}, u32[]{:S(2)}, u32[]{:S(2)}) %collective-permute-start.2) | collective-permute-done | bytes 524320 | tf_op jit(solution)/shard_map/kernel_exchange/ppermute | solution.py:266
  71.7 0.8 copy-done.6
  72.5 0.8 copy-done.7
  73.3 0.0 collective-permute-done.4.refs_5_
  73.3 0.0 all-to-all-done
  73.4 5.4 %shard_map.74 = bf16[256,128]{1,0:T(8,128)(2,1)S(1)} custom-call(s32[1]{0:T(128)} %bitcast.me_ref, bf16[2048,128]{1,0:T(8,128)(2,1)S(1)} %bitcast.51, bf16[512,1024]{1,0:T(8,128)(2,1)} %constant.55.clone.fwd_ref, bf16[1024,512]{1,0:T(8,128)(2,1)} %constant.56.clone.inv_ref, bf16[64,16,256]{2,1,0:T(8,128)(2,1)S(1)} %get-tuple-element.17.cut_ref.refs_0_, ...), custom_call_target="tpu_custom_call" | custom-call | flops 1000000000 | bytes 6815748 | tf_op jit(solution)/shard_map/pallas_call | solution.py:229
  78.7 13.4 %all_to_all.66 = bf16[32,8,128]{2,1,0:T(8,128)(2,1)S(1)} all-to-all(bf16[32,8,128]{2,1,0:T(8,128)(2,1)S(1)} %bitcast.59), channel_id=1, replica_groups=mesh['xl'=2,'zh'=4,'zl'=2,'yh'=2,'yl'=2,'xh'=2,'c'=2] {'xh','c','xl','zl..., dimensions={0} | all-to-all | bytes 131072 | tf_op jit(solution)/shard_map/to_rows/all_to_all | solution.py:298
  92.1 0.4 shard_map.75
  92.5 32.3 %all_to_all.67 = bf16[256,8,128]{2,1,0:T(8,128)(2,1)S(1)} all-to-all(bf16[256,8,128]{2,1,0:T(8,128)(2,1)S(1)} %bitcast.49), channel_id=1, replica_groups=mesh['xl'=2,'zh'=4,'zl'=2,'yh'=2,'yl'=2,'xh'=2,'c'=2] {'xh','c','xl','zh..., dimensions={0} | all-to-all | bytes 1048576 | tf_op jit(solution)/shard_map/to_wavenumbers/all_to_all | solution.py:280
  124.8 5.4 %shard_map.76 = bf16[256,128]{1,0:T(8,128)(2,1)S(1)} custom-call(s32[1]{0:T(128)} %bitcast.me_ref, bf16[2048,128]{1,0:T(8,128)(2,1)S(1)} %bitcast.53, bf16[512,1024]{1,0:T(8,128)(2,1)} %constant.55.clone.fwd_ref, bf16[1024,512]{1,0:T(8,128)(2,1)} %constant.56.clone.inv_ref, bf16[64,16,256]{2,1,0:T(8,128)(2,1)S(1)} %get-tuple-element.17.cut_ref.refs_0_, ...), custom_call_target="tpu_custom_call" | custom-call | flops 1000000000 | bytes 6815748 | tf_op jit(solution)/shard_map/pallas_call | solution.py:229
  130.2 10.6 %all_to_all.68 = bf16[32,8,128]{2,1,0:T(8,128)(2,1)S(1)} all-to-all(bf16[32,8,128]{2,1,0:T(8,128)(2,1)S(1)} %bitcast.60), channel_id=1, replica_groups=mesh['xl'=2,'zh'=4,'zl'=2,'yh'=2,'yl'=2,'xh'=2,'c'=2] {'xh','c','xl','zl..., dimensions={0} | all-to-all | bytes 131072 | tf_op jit(solution)/shard_map/to_rows/all_to_all | solution.py:298
  140.9 0.4 shard_map.77
  141.3 26.4 %all_to_all.69 = bf16[256,8,128]{2,1,0:T(8,128)(2,1)S(1)} all-to-all(bf16[256,8,128]{2,1,0:T(8,128)(2,1)S(1)} %bitcast.50), channel_id=1, replica_groups=mesh['xl'=2,'zh'=4,'zl'=2,'yh'=2,'yl'=2,'xh'=2,'c'=2] {'xh','c','xl','zh..., dimensions={0} | all-to-all | bytes 1048576 | tf_op jit(solution)/shard_map/to_wavenumbers/all_to_all | solution.py:280
  167.7 5.4 %shard_map.78 = bf16[256,128]{1,0:T(8,128)(2,1)S(1)} custom-call(s32[1]{0:T(128)} %bitcast.me_ref, bf16[2048,128]{1,0:T(8,128)(2,1)S(1)} %bitcast.52, bf16[512,1024]{1,0:T(8,128)(2,1)} %constant.55.clone.fwd_ref, bf16[1024,512]{1,0:T(8,128)(2,1)} %constant.56.clone.inv_ref, bf16[64,16,256]{2,1,0:T(8,128)(2,1)S(1)} %get-tuple-element.17.cut_ref.refs_0_, ...), custom_call_target="tpu_custom_call" | custom-call | flops 1000000000 | bytes 6815748 | tf_op jit(solution)/shard_map/pallas_call | solution.py:229
  173.1 10.7 %all_to_all.70 = bf16[32,8,128]{2,1,0:T(8,128)(2,1)S(1)} all-to-all(bf16[32,8,128]{2,1,0:T(8,128)(2,1)S(1)} %bitcast.58), channel_id=1, replica_groups=mesh['xl'=2,'zh'=4,'zl'=2,'yh'=2,'yl'=2,'xh'=2,'c'=2] {'xh','c','xl','zl..., dimensions={0} | all-to-all | bytes 131072 | tf_op jit(solution)/shard_map/to_rows/all_to_all | solution.py:298
  183.7 0.8 shard_map.79
  (15 shorter events, 0.0 us)
Async XLA Ops:
  0.0 11.6 %copy-start = (bf16[256,256]{1,0:T(8,128)(2,1)S(1)}, bf16[256,256]{1,0:T(8,128)(2,1)}, u32[]{:S(2)}) copy-start(bf16[256,256]{1,0:T(8,128)(2,1)} %constant.54.clone.table_ref.inv_ref) | copy-start | bytes 393220
  0.0 11.6 %copy-start.1 = (f32[1,2,2,32,128]{4,3,2,1,0:T(8,128)S(1)}, f32[1,2,2,32,128]{4,3,2,1,0:T(8,128)}, u32[]{:S(2)}) copy-start(f32[1,2,2,32,128]{4,3,2,1,0:T(8,128)} %param.7) | copy-start | bytes 196612
  0.0 11.6 %copy-start.2 = (f32[1,32,128]{2,1,0:T(8,128)S(1)}, f32[1,32,128]{2,1,0:T(8,128)}, u32[]{:S(2)}) copy-start(f32[1,32,128]{2,1,0:T(8,128)} %param.8) | copy-start | bytes 49156
  3.8 26.6 %collective-permute-start.6 = (bf16[64,16,256]{2,1,0:T(8,128)(2,1)}, bf16[64,16,256]{2,1,0:T(8,128)(2,1)S(1)}, u32[]{:S(2)}, u32[]{:S(2)}) collective-permute-start(bf16[64,16,256]{2,1,0:T(8,128)(2,1)} %dynamic-slice_bitcast_fusion.6), channel_id=1, source_target_pairs={{0,148},{4,144},{16,132},{20,128},{128,20},{132,16},{144,4},{148,0... | collective-permute-start | bytes 1572872 | tf_op jit(solution)/shard_map/kernel_exchange/ppermute | solution.py:266
  8.2 23.5 %collective-permute-start.5 = (bf16[64,16,256]{2,1,0:T(8,128)(2,1)}, bf16[64,16,256]{2,1,0:T(8,128)(2,1)S(1)}, u32[]{:S(2)}, u32[]{:S(2)}) collective-permute-start(bf16[64,16,256]{2,1,0:T(8,128)(2,1)} %dynamic-slice_bitcast_fusion.7), channel_id=1, source_target_pairs={{0,144},{4,148},{16,128},{20,132},{128,16},{132,20},{144,0},{148,4... | collective-permute-start | bytes 1572872 | tf_op jit(solution)/shard_map/kernel_exchange/ppermute | solution.py:266
  12.6 60.7 %all-to-all-start = ((bf16[256,8,128]{2,1,0:T(8,128)(2,1)}), bf16[256,8,128]{2,1,0:T(8,128)(2,1)S(1)}, u32[]{:S(2)}, u32[]{:S(2)}) async-start(bf16[256,8,128]{2,1,0:T(8,128)(2,1)} %bitcast.12), calls=%async_computation | async-start | bytes 1048576 | tf_op jit(solution)/shard_map/to_wavenumbers/all_to_all | solution.py:280
  27.6 17.3 %collective-permute-start = (bf16[64,16,256]{2,1,0:T(8,128)(2,1)}, bf16[64,16,256]{2,1,0:T(8,128)(2,1)S(1)}, u32[]{:S(2)}, u32[]{:S(2)}) collective-permute-start(bf16[64,16,256]{2,1,0:T(8,128)(2,1)} %get-tuple-element.18), channel_id=1, source_target_pairs={{0,4},{4,0},{16,20},{20,16},{128,132},{132,128},{144,148},{148,144... | collective-permute-start | bytes 1572872 | tf_op jit(solution)/shard_map/kernel_exchange/ppermute | solution.py:266
  29.0 24.4 %collective-permute-start.1 = (bf16[64,16,256]{2,1,0:T(8,128)(2,1)}, bf16[64,16,256]{2,1,0:T(8,128)(2,1)S(1)}, u32[]{:S(2)}, u32[]{:S(2)}) collective-permute-start(bf16[64,16,256]{2,1,0:T(8,128)(2,1)} %get-tuple-element.19), channel_id=1, source_target_pairs={{0,16},{4,20},{16,0},{20,4},{128,144},{132,148},{144,128},{148,132... | collective-permute-start | bytes 1572872 | tf_op jit(solution)/shard_map/kernel_exchange/ppermute | solution.py:266
  30.4 41.3 %collective-permute-start.2 = (bf16[64,16,256]{2,1,0:T(8,128)(2,1)}, bf16[64,16,256]{2,1,0:T(8,128)(2,1)S(1)}, u32[]{:S(2)}, u32[]{:S(2)}) collective-permute-start(bf16[64,16,256]{2,1,0:T(8,128)(2,1)} %get-tuple-element.20), channel_id=1, source_target_pairs={{0,20},{4,16},{16,4},{20,0},{128,148},{132,144},{144,132},{148,128... | collective-permute-start | bytes 1572872 | tf_op jit(solution)/shard_map/kernel_exchange/ppermute | solution.py:266
  30.4 42.9 %copy-start.3 = (bf16[64,16,256]{2,1,0:T(8,128)(2,1)}, bf16[64,16,256]{2,1,0:T(8,128)(2,1)S(1)}, u32[]{:S(2)}) copy-start(bf16[64,16,256]{2,1,0:T(8,128)(2,1)S(1)} %collective-permute-done.6.refs_7_) | copy-start | bytes 1572868
  30.4 41.3 %collective-permute-start.3 = (bf16[64,16,256]{2,1,0:T(8,128)(2,1)}, bf16[64,16,256]{2,1,0:T(8,128)(2,1)S(1)}, u32[]{:S(2)}, u32[]{:S(2)}) collective-permute-start(bf16[64,16,256]{2,1,0:T(8,128)(2,1)} %get-tuple-element.21), channel_id=1, source_target_pairs={{0,128},{4,132},{16,144},{20,148},{128,0},{132,4},{144,16},{148,20... | collective-permute-start | bytes 1572872 | tf_op jit(solution)/shard_map/kernel_exchange/ppermute | solution.py:266
  31.7 41.6 %copy-start.4 = (bf16[64,16,256]{2,1,0:T(8,128)(2,1)}, bf16[64,16,256]{2,1,0:T(8,128)(2,1)S(1)}, u32[]{:S(2)}) copy-start(bf16[64,16,256]{2,1,0:T(8,128)(2,1)S(1)} %collective-permute-done.5.refs_6_) | copy-start | bytes 1572868
  31.7 41.6 %collective-permute-start.4 = (bf16[64,16,256]{2,1,0:T(8,128)(2,1)}, bf16[64,16,256]{2,1,0:T(8,128)(2,1)}, u32[]{:S(2)}, u32[]{:S(2)}) collective-permute-start(bf16[64,16,256]{2,1,0:T(8,128)(2,1)} %get-tuple-element.22), channel_id=1, source_target_pairs={{0,132},{4,128},{16,148},{20,144},{128,4},{132,0},{144,20},{148,16... | collective-permute-start | bytes 1572872 | tf_op jit(solution)/shard_map/kernel_exchange/ppermute | solution.py:266
  53.5 19.9 %copy-start.5 = (bf16[64,16,256]{2,1,0:T(8,128)(2,1)}, bf16[64,16,256]{2,1,0:T(8,128)(2,1)S(1)}, u32[]{:S(2)}) copy-start(bf16[64,16,256]{2,1,0:T(8,128)(2,1)S(1)} %collective-permute-done.1.refs_2_) | copy-start | bytes 1572868
  71.7 0.8 copy-start.6
  72.5 0.8 copy-start.7
